TPU v7x, 512 devices: a whole 4x8x8 slice. The times are simulated.
512 devices in a mesh: season: 8 (over y), row: 8 (over z_lo, x), col: 8 (over z_hi, core).
Axes of the slice: x: 4, y: 8, z: 8 (z_hi: 4, z_lo: 2; z = z_hi * 2 + z_lo), core: 2. Of those that a mesh axis runs over, the one named last changes fastest.
Arguments:
- tiles: float32 [8, 8, 8, 32, 128, 128], P('season', 'row', 'col'), may hold values from -0.125 to 0.125
- tile_rows: int32 [8, 8, 8, 32], P('season', 'row', 'col'), may hold values from 0 to 15, as said below
- tile_cols: int32 [8, 8, 8, 32], P('season', 'row', 'col'), may hold values from 0 to 15, as said below
- rhs: float32 [8, 16384], P('season', 'row')
- coupling: float32 [8, 16384], P('season', 'row'), may hold values from -1 to -0.2
- asset: int32 [8, 16384], P('season', 'row'), may hold values from 0 to 65535
- cost_x: float32 [8, 16384], P('season', 'col'), may hold values from -6 to 6
- upper: float32 [8, 16384], P('season', 'col'), may hold values from 0.5 to 4
- cost_z: float32 [65536], replicated, may hold values from 0.2 to 2
- x_init: float32 [8, 16384], P('season', 'col'), may hold values from 0 to 1
- z_init: float32 [65536], replicated, may hold values from 0 to 1
- y_init: float32 [8, 16384], P('season', 'row'), may hold values from 0 to 1
Outputs:
- x_final: float32 [8, 16384], P('season', 'col')
- z_final: float32 [65536], replicated
- y_final: float32 [8, 16384], P('season', 'row')
Inputs may be any that keep to these rules, and one draw needn't show every extreme that they name: `tile_rows`: within each device's part, the tiles sit at distinct positions, and every block row and every block column holds exactly two tiles. `tile_cols`: see tile_rows: every block column of a device's part holds exactly two tiles.
All inputs are finite; a program needn't handle non-finite values.
Results may differ from a plain program's by a relative error of at most 0.0003.
Values sent between devices are 32-bit elements; how exact they have to be, the bound alone decides.
A program may use at most 64 MiB of HBM per device.

v0:
```python
import jax
import jax.numpy as jnp
from jax import lax
from jax.sharding import PartitionSpec as P

ITERS = 3


STEP_SCALE = 0.35
EPSILON = 1e-06


def forward_tiles(tile_vals, row_hot, col_hot, values):
    blocks = values.reshape(col_hot.shape[1], -1)
    picked = jnp.dot(col_hot, blocks, precision=lax.Precision.HIGHEST)
    product = jnp.einsum("ktu,ku->kt", tile_vals, picked, precision=lax.Precision.HIGHEST)
    return jnp.dot(row_hot.T, product, precision=lax.Precision.HIGHEST).reshape(-1)


def backward_tiles(tile_vals, row_hot, col_hot, values):
    blocks = values.reshape(row_hot.shape[1], -1)
    picked = jnp.dot(row_hot, blocks, precision=lax.Precision.HIGHEST)
    product = jnp.einsum("ktu,kt->ku", tile_vals, picked, precision=lax.Precision.HIGHEST)
    return jnp.dot(col_hot.T, product, precision=lax.Precision.HIGHEST).reshape(-1)


def local(
    tiles, tile_rows, tile_cols, rhs, coupling, asset, cost_x, upper, cost_z, x_init, z_init, y_init
):
    tile_vals = tiles.reshape(tiles.shape[3:])
    width = rhs.shape[1]
    blocks_dev = width // tile_vals.shape[1]
    row_hot = (tile_rows.reshape(-1)[:, None] == jnp.arange(blocks_dev)[None, :]).astype(
        jnp.float32
    )
    col_hot = (tile_cols.reshape(-1)[:, None] == jnp.arange(blocks_dev)[None, :]).astype(
        jnp.float32
    )
    demand = rhs.reshape(-1)
    couple = coupling.reshape(-1)
    assets = asset.reshape(-1)
    prices = cost_x.reshape(-1)
    bounds = upper.reshape(-1)
    primal = x_init.reshape(-1)
    invest = z_init
    duals = y_init.reshape(-1)
    n_inv = cost_z.shape[0]
    balance = jnp.float32(1.0)
    capacity = jnp.zeros((n_inv,), jnp.float32)
    for iteration in range(ITERS):
        primal_step = STEP_SCALE / balance
        dual_step = STEP_SCALE * balance
        capacity = lax.psum(
            jax.ops.segment_sum(couple * duals, assets, num_segments=n_inv), ("season", "row")
        )
        new_z = jnp.maximum(invest - primal_step * (cost_z - capacity), 0.0)
        transposed = lax.psum(backward_tiles(tile_vals, row_hot, col_hot, duals), "row")
        new_x = jnp.clip(primal - primal_step * (prices - transposed), 0.0, bounds)
        extra_x = 2.0 * new_x - primal
        extra_z = 2.0 * new_z - invest
        linked = couple * extra_z[assets]
        image = lax.psum(forward_tiles(tile_vals, row_hot, col_hot, extra_x), "col")
        new_y = jnp.maximum(duals + dual_step * (demand - (image + linked)), 0.0)
        if iteration + 1 < ITERS:
            primal_local = jnp.sum((new_x - primal) ** 2)
            dual_local = jnp.sum((new_y - duals) ** 2)
            invest_sq = jnp.sum((new_z - invest) ** 2)
            primal_sq = lax.psum(primal_local, ("season", "col")) + invest_sq
            dual_sq = lax.psum(dual_local, ("season", "row"))
            balance = jnp.sqrt(balance * jnp.sqrt((primal_sq + EPSILON) / (dual_sq + EPSILON)))
        primal, invest, duals = (new_x, new_z, new_y)
    return (primal.reshape(1, -1), invest, duals.reshape(1, -1))


def solution(mesh):
    in_specs = (
        P("season", "row", "col", None, None, None),
        P("season", "row", "col", None),
        P("season", "row", "col", None),
        P("season", "row"),
        P("season", "row"),
        P("season", "row"),
        P("season", "col"),
        P("season", "col"),
        P(),
        P("season", "col"),
        P(),
        P("season", "row"),
    )
    out_specs = (P("season", "col"), P(), P("season", "row"))
    return jax.shard_map(local, mesh=mesh, in_specs=in_specs, out_specs=out_specs, check_vma=False)
```

profile of v0, /device:TPU:1, one launch (start us, length us, event | category | flops | bytes accessed | tf_op | source)
XLA Modules:
  0.0 2363.8 jit_solution(7211275562511703066)
XLA Ops:
  8.1 12.1 scatter_custom_fusion
  24.0 17.8 psum.91
  42.7 3.4 fusion.8
  46.3 23.1 psum.94
  69.5 485.1 %all-reduce.4.cloned.1.call-done = f32[65536]{0:T(1024)} async-done(((f32[65536]{0:T(1024)}), f32[65536]{0:T(1024)}) %all-reduce.4.cloned.1.call-update) | async-done | bytes 262160 | tf_op jit(solution)/shard_map/psum | solution.py:53
  556.2 11.8 gather_fusion
  568.7 167.6 %psum.92 = f32[]{:T(128)} all-reduce(f32[]{:T(128)} %get-tuple-element.15), channel_id=1, replica_groups=mesh['season'=8,'row'=8,'col'=8] {'season','col'}, use_global_device_ids=true, to_apply=%region_2.0 | all-reduce | flops 1 | bytes 8 | tf_op jit(solution)/shard_map/psum | solution.py:68
  736.3 125.1 %psum.95 = f32[]{:T(128)} all-reduce(f32[]{:T(128)} %multiply_reduce_fusion.4), channel_id=1, replica_groups=mesh['season'=8,'row'=8,'col'=8] {'season','row'}, use_global_device_ids=true, to_apply=%region_8.9 | all-reduce | flops 1 | bytes 8 | tf_op jit(solution)/shard_map/psum | solution.py:69
  863.7 1.9 fusion.6
  865.9 14.3 psum.96
  880.8 170.8 %psum.97 = f32[]{:T(128)} all-reduce(f32[]{:T(128)} %get-tuple-element.9), channel_id=1, replica_groups=mesh['season'=8,'row'=8,'col'=8] {'season','col'}, use_global_device_ids=true, to_apply=%region_11.12 | all-reduce | flops 1 | bytes 8 | tf_op jit(solution)/shard_map/psum | solution.py:68
  1051.7 12.1 scatter_custom_fusion.1
  1064.1 3.4 fusion.4
  1067.7 14.4 psum.99
  1082.1 501.9 %all-reduce.6.cloned.1.call-done = f32[65536]{0:T(1024)} async-done(((f32[65536]{0:T(1024)}), f32[65536]{0:T(1024)}) %all-reduce.6.cloned.1.call-update) | async-done | bytes 262160 | tf_op jit(solution)/shard_map/psum | solution.py:53
  1585.7 11.8 gather_fusion.1
  1599.4 129.7 %psum.100 = f32[]{:T(128)} all-reduce(f32[]{:T(128)} %multiply_reduce_fusion.2), channel_id=1, replica_groups=mesh['season'=8,'row'=8,'col'=8] {'season','row'}, use_global_device_ids=true, to_apply=%region_17.18 | all-reduce | flops 1 | bytes 8 | tf_op jit(solution)/shard_map/psum | solution.py:69
  1730.1 1.9 fusion.2
  1732.2 13.0 psum.101
  1745.4 12.1 scatter_custom_fusion.2
  1757.5 3.4 fusion
  1761.1 72.8 %psum.103 = f32[2048]{0:T(1024)S(1)} all-reduce(f32[2048]{0:T(1024)S(1)} %convolution_bitcast_fusion), channel_id=1, replica_groups=mesh['season'=8,'row'=8,'col'=8] {'col'}, use_global_device_ids=true, to_apply=%region_21.22 | all-reduce | flops 2048 | bytes 16384 | tf_op jit(solution)/shard_map/psum | solution.py:62
  1834.0 509.1 %all-reduce.8.cloned.1.call-done = f32[65536]{0:T(1024)} async-done(((f32[65536]{0:T(1024)}), f32[65536]{0:T(1024)}) %all-reduce.8.cloned.1.call-update) | async-done | bytes 262160 | tf_op jit(solution)/shard_map/psum | solution.py:53
  2344.8 11.8 gather_fusion.2
  (59 shorter events, 15.3 us)
Async XLA Ops:
  7.2 14.7 copy-start
  7.2 16.6 copy-start.10
  7.2 34.7 %copy-start.8 = (f32[1,2048]{1,0:T(1,128)S(1)}, f32[1,2048]{1,0:T(1,128)}, u32[]{:S(2)}) copy-start(f32[1,2048]{1,0:T(1,128)} %param.21) | copy-start | bytes 24580
  7.2 34.7 %copy-start.6 = (f32[1,2048]{1,0:T(1,128)S(1)}, f32[1,2048]{1,0:T(1,128)}, u32[]{:S(2)}) copy-start(f32[1,2048]{1,0:T(1,128)} %param.19) | copy-start | bytes 24580
  7.2 34.7 %copy-start.7 = (f32[1,2048]{1,0:T(1,128)S(1)}, f32[1,2048]{1,0:T(1,128)}, u32[]{:S(2)}) copy-start(f32[1,2048]{1,0:T(1,128)} %param.18) | copy-start | bytes 24580
  7.2 547.3 %all-reduce.4.cloned.1.call-start = ((), (), s32[]{:S(2)}) async-start(), calls=%async_computation | async-start | bytes 524288 | tf_op jit(solution)/shard_map/psum | solution.py:53
  20.2 1563.9 %all-reduce.6.cloned.1.call-start = ((), (), s32[]{:S(2)}) async-start(), calls=%async_computation.1 | async-start | bytes 524288 | tf_op jit(solution)/shard_map/psum | solution.py:53
  21.9 24.2 %copy-start.11 = (s32[1,1,1,32]{3,2,1,0:T(1,128)S(1)}, s32[1,1,1,32]{3,2,1,0:T(1,128)}, u32[]{:S(2)}) copy-start(s32[1,1,1,32]{3,2,1,0:T(1,128)} %param.13) | copy-start | bytes 388
  21.9 532.7 %copy-start.1 = (f32[65536]{0:T(1024)S(1)}, f32[65536]{0:T(1024)}, u32[]{:S(2)}) copy-start(f32[65536]{0:T(1024)} %param.20) | copy-start | bytes 786436
  21.9 532.6 %copy-start.2 = (f32[65536]{0:T(1024)S(1)}, f32[65536]{0:T(1024)}, u32[]{:S(2)}) copy-start(f32[65536]{0:T(1024)} %param.22) | copy-start | bytes 786436
  556.2 11.8 copy-start.3
  556.2 11.8 copy-start.4
  556.2 11.8 copy-start.5
  1063.8 1279.3 %all-reduce.8.cloned.1.call-start = ((), (), s32[]{:S(2)}) async-start(), calls=%async_computation.2 | async-start | bytes 524288 | tf_op jit(solution)/shard_map/psum | solution.py:53
  1745.2 611.4 %copy-start.9 = (f32[2048]{0:T(1024)}, f32[2048]{0:T(1024)S(1)}, u32[]{:S(2)}) copy-start(f32[2048]{0:T(1024)S(1)} %maximum_minimum_fusion) | copy-start | bytes 24580
Sparse Core Ops, SparseCore 0:
  20.3 534.1 all-reduce.3
  1064.0 520.0 all-reduce.5
  1757.6 585.4 all-reduce.7
where the time goes:
time: 2390 us; the launch traced here: 2360 us
  waiting for transfers between devices  1500 us (63%)
  blocking collectives  749 us (31%)
  other arithmetic  45.9 us (2%)
  local copies, waits for them, and re-layouts  35.4 us (1%)
    psum x3, waiting for transfers between devices, local(): lax.psum(jax.ops.segment_sum(couple * duals, assets, num_segments=n_inv),...  1500 us
    psum x2, blocking collectives, local(): primal_sq = lax.psum(primal_local, ('season', 'col')) + invest_sq  338 us
    psum x2, blocking collectives, local(): dual_sq = lax.psum(dual_local, ('season', 'row'))  255 us
    psum x3, blocking collectives, local(): image = lax.psum(forward_tiles(tile_vals, row_hot, col_hot, extra_x), 'col')  110 us
  transfers between devices with their start and end apart: 3, of which 3 were waited for; matrix products, arithmetic and copies ran while one was open for 1% of the time, Pallas kernels for 0%

commit v1 on v0

v1 whole, which is shorter than its diff:
```python
import functools

import jax
import jax.numpy as jnp
from jax import lax
from jax.experimental import pallas as pl
from jax.experimental.pallas import tpu as pltpu
from jax.sharding import PartitionSpec as P

ITERS = 3
STEP_SCALE = 0.35
EPSILON = 1e-06

MESH = pl.DeviceIdType.MESH
F32, BF16, I32 = jnp.float32, jnp.bfloat16, jnp.int32
G = 8
NB = 16
TILE = 128
TILES = 32
CH = 64
SUB = CH // G


def peer(axis, k):
    return {axis: lax.rem(lax.axis_index(axis) + k, G)}


def to_peers(axis, copy):
    for k in range(1, G):
        copy(lax.rem(lax.axis_index(axis) + k, G), peer(axis, k))


def wait_bytes(ref, sem):
    pltpu.make_async_copy(ref, ref, sem).wait()


def split2(v):
    high = v.astype(BF16)
    return high, (v - high.astype(F32)).astype(BF16)


def first_and_last(keys, other):
    k = lax.broadcasted_iota(I32, (NB, TILES), 1)
    hit = keys == lax.broadcasted_iota(I32, (NB, TILES), 0)
    one = jnp.min(jnp.where(hit, k, TILES - 1), axis=1, keepdims=True)
    two = jnp.max(jnp.where(hit, k, 0), axis=1, keepdims=True)
    pick = lambda t: jnp.sum(jnp.where(k == t, other, 0), axis=1, keepdims=True)
    return one, two, pick(one), pick(two)


def products(order, column, tiles_ref, values_ref, picked, out):
    for b in range(NB):
        picked[b : b + 1, 0:TILE] = values_ref[pl.ds(order[b, column + 2], 1), :]
        picked[b : b + 1, TILE : 2 * TILE] = values_ref[pl.ds(order[b, column + 3], 1), :]
    high, low = split2(picked[...])
    left = jnp.concatenate([high, low], axis=0)
    for b in range(NB):
        right = jnp.concatenate(
            [tiles_ref[order[b, column]], tiles_ref[order[b, column + 1]]], axis=0
        )
        res = jnp.dot(left, right, preferred_element_type=F32)
        row = res[b : b + 1, :] + res[NB + b : NB + b + 1, :]
        out(b, row[:, 0:TILE] + row[:, TILE : 2 * TILE])


def kernel(
    tiles_hbm, rows_ref, cols_ref, rhs_ref, coup_ref, asset_ref, costx_ref, upper_ref, costz_hbm, x0_ref, z0_hbm, y0_ref,
    x_out, z_out, y_out,
    tiles, tb, tf, costz, zv, xv, yv, tr, fw, picked, order_v, order, hot_hi, hot_lo, left,
    gsend, rs, rx, sx, ez, cx, zall,
    load_sem, order_sem, send_sem, recv_sem, zs_sem, zr_sem,
):
    s, r, c = (lax.axis_index(a) for a in ("season", "row", "col"))
    barrier = pltpu.get_barrier_semaphore()
    for axis in ("season", "row", "col"):
        for k in range(1, G):
            pl.semaphore_signal(barrier, inc=1, device_id=peer(axis, k), device_id_type=MESH)
    mine = pl.ds(pl.multiple_of(c * CH + r * SUB, SUB), SUB)
    loads = [
        pltpu.make_async_copy(costz_hbm.at[mine], costz, load_sem.at[0]),
        pltpu.make_async_copy(z0_hbm.at[mine], zv, load_sem.at[1]),
        pltpu.make_async_copy(tiles_hbm, tiles, load_sem.at[2]),
    ]
    for load in loads:
        load.start()

    rows, cols = rows_ref[...], cols_ref[...]
    place = lax.broadcasted_iota(I32, (NB, TILE), 1)
    table = jnp.zeros((NB, TILE), I32)
    for at, col in enumerate(first_and_last(cols, rows) + first_and_last(rows, cols)):
        table = jnp.where(place == at, col, table)
    order_v[...] = table
    to_smem = pltpu.make_async_copy(order_v, order, order_sem)
    to_smem.start()

    asset = asset_ref[...]
    low, high = asset & (TILE - 1), (asset >> 7) - c * CH
    for n in range(NB):
        at = slice(n * TILE, (n + 1) * TILE)
        hit = lax.broadcasted_iota(I32, (TILE, TILE), 0) == low[n : n + 1, :]
        one = jnp.where(hit, 1.0, 0.0).astype(BF16)
        hot_lo[0:TILE, at] = one
        hot_lo[TILE : 2 * TILE, at] = one
        hit = lax.broadcasted_iota(I32, (CH, TILE), 0) == high[n : n + 1, :]
        hot_hi[:, at] = jnp.where(hit, 1.0, 0.0).astype(BF16)

    coup = coup_ref[...]
    xv[...] = x0_ref[...]
    yv[...] = y0_ref[...]
    balance = None
    stats = None
    for it in range(ITERS):
        last = it + 1 == ITERS
        srows = SUB if it == 0 else SUB + 2
        crows = NB if last else NB + 1
        sem = lambda phase: (send_sem.at[it, phase], recv_sem.at[it, phase])

        v_high, v_low = split2(coup * yv[...])
        for n in range(NB):
            at = slice(n * TILE, (n + 1) * TILE)
            hot = hot_hi[:, at]
            left[0:CH, at] = hot * v_high[n : n + 1, :]
            left[CH : 2 * CH, at] = hot * v_low[n : n + 1, :]
        cap = lax.dot_general(
            left[...], hot_lo[0:TILE, :], (((1,), (1,)), ((), ())), preferred_element_type=F32
        )
        cap = cap[0:CH] + cap[CH : 2 * CH]
        for k in range(G):
            gsend[it, k, 0:SUB] = cap[k * SUB : (k + 1) * SUB]
            if it:
                gsend[it, k, SUB : SUB + 2] = stats
        if it == 0:
            pl.semaphore_wait(barrier, 3 * (G - 1))
        sends, recvs = sem(0)

        def send(to, device):
            pltpu.make_async_remote_copy(
                src_ref=gsend.at[it, to, pl.ds(0, srows)], dst_ref=rs.at[it, r, pl.ds(0, srows)],
                send_sem=sends, recv_sem=recvs, device_id=device, device_id_type=MESH,
            ).start()

        to_peers("row", send)
        rs[it, r] = gsend[it, r]

        if it == 0:
            to_smem.wait()
            loads[2].wait()
            for k in range(TILES):
                t_high, t_low = split2(tiles[k])
                tb[k, :, 0:TILE] = t_high
                tb[k, :, TILE : 2 * TILE] = t_low

        def put(b, row):
            rx[it, r, b : b + 1, :] = row

        products(order, 0, tb, yv, picked, put)
        x_sends, x_recvs = sem(1)

        def send(to, device):
            pltpu.make_async_remote_copy(
                src_ref=rx.at[it, r], dst_ref=rx.at[it, r],
                send_sem=x_sends, recv_sem=x_recvs, device_id=device, device_id_type=MESH,
            ).start()

        to_peers("row", send)

        wait_bytes(rs.at[it, pl.ds(0, G - 1), pl.ds(0, srows)], recvs)
        sx[it, s, 0:srows] = jnp.sum(rs[it, :, 0:srows], axis=0)
        sends, recvs = sem(2)

        def send(to, device):
            pltpu.make_async_remote_copy(
                src_ref=sx.at[it, s, pl.ds(0, srows)], dst_ref=sx.at[it, s, pl.ds(0, srows)],
                send_sem=sends, recv_sem=recvs, device_id=device, device_id_type=MESH,
            ).start()

        to_peers("season", send)
        if it == 0:
            for k in range(TILES):
                t_high, t_low = split2(tiles[k].T)
                tf[k, :, 0:TILE] = t_high
                tf[k, :, TILE : 2 * TILE] = t_low
            loads[0].wait()
            loads[1].wait()
        wait_bytes(rx.at[it, pl.ds(0, G - 1)], x_recvs)
        transposed = jnp.sum(rx[it], axis=0)
        wait_bytes(sx.at[it, pl.ds(0, G - 1), pl.ds(0, srows)], recvs)
        total = jnp.sum(sx[it, :, 0:srows], axis=0)
        if it == 0:
            primal_step, dual_step = jnp.full((1, 1), STEP_SCALE, F32), jnp.full((1, 1), STEP_SCALE, F32)
        else:
            dual_sq = jnp.sum(total[SUB : SUB + 1], axis=1, keepdims=True)
            primal_sq = jnp.sum(total[SUB + 1 : SUB + 2], axis=1, keepdims=True) * (1.0 / G)
            root = jnp.sqrt((primal_sq + EPSILON) / (dual_sq + EPSILON))
            balance = jnp.sqrt(root if balance is None else balance * root)
            primal_step, dual_step = STEP_SCALE / balance, STEP_SCALE * balance

        z_old = zv[...]
        z_new = jnp.maximum(z_old - primal_step * (costz[...] - total[0:SUB]), 0.0)
        zv[...] = z_new
        ez[it, r] = 2.0 * z_new - z_old
        sends, recvs = sem(3)

        def send(to, device):
            pltpu.make_async_remote_copy(
                src_ref=ez.at[it, r], dst_ref=ez.at[it, r],
                send_sem=sends, recv_sem=recvs, device_id=device, device_id_type=MESH,
            ).start()

        to_peers("row", send)
        if last:
            zall[c, r] = z_new

            def send(to, device):
                pltpu.make_async_remote_copy(
                    src_ref=zall.at[c, r], dst_ref=zall.at[c, r],
                    send_sem=zs_sem.at[0], recv_sem=zr_sem.at[0], device_id=device, device_id_type=MESH,
                ).start()

            to_peers("row", send)

        x_old = xv[...]
        x_new = jnp.clip(x_old - primal_step * (costx_ref[...] - transposed), 0.0, upper_ref[...])
        xv[...] = x_new
        tr[...] = 2.0 * x_new - x_old

        def put(b, row):
            fw[b : b + 1, :] = row

        products(order, 4, tf, tr, picked, put)
        if last:
            x_out[...] = x_new
            wait_bytes(zall.at[0, pl.ds(0, G - 1)], zr_sem.at[0])
        else:
            cx[it, c, NB : NB + 1] = jnp.sum((x_new - x_old) ** 2, axis=0, keepdims=True) + jnp.sum(
                (z_new - z_old) ** 2, axis=0, keepdims=True
            )

        wait_bytes(ez.at[it, pl.ds(0, G - 1)], recvs)
        e_high, e_low = split2(ez[it].reshape(CH, TILE))
        gathered = jnp.dot(
            jnp.concatenate([e_high, e_low], axis=1), hot_lo[...], preferred_element_type=F32
        )
        for n in range(NB):
            at = slice(n * TILE, (n + 1) * TILE)
            linked = jnp.sum(gathered[:, at] * hot_hi[:, at].astype(F32), axis=0, keepdims=True)
            cx[it, c, n : n + 1] = fw[n : n + 1, :] + coup[n : n + 1, :] * linked
        sends, recvs = sem(4)

        def send(to, device):
            pltpu.make_async_remote_copy(
                src_ref=cx.at[it, c, pl.ds(0, crows)], dst_ref=cx.at[it, c, pl.ds(0, crows)],
                send_sem=sends, recv_sem=recvs, device_id=device, device_id_type=MESH,
            ).start()

        to_peers("col", send)
        if last:

            def send(to, device):
                pltpu.make_async_remote_copy(
                    src_ref=zall.at[c], dst_ref=zall.at[c],
                    send_sem=zs_sem.at[1], recv_sem=zr_sem.at[1], device_id=device, device_id_type=MESH,
                ).start()

            to_peers("col", send)
        wait_bytes(cx.at[it, pl.ds(0, G - 1), pl.ds(0, crows)], recvs)
        image = jnp.sum(cx[it, :, 0:crows], axis=0)

        y_old = yv[...]
        y_new = jnp.maximum(y_old + dual_step * (rhs_ref[...] - image[0:NB]), 0.0)
        yv[...] = y_new
        if last:
            y_out[...] = y_new
        else:
            stats = jnp.concatenate(
                [jnp.sum((y_new - y_old) ** 2, axis=0, keepdims=True), image[NB : NB + 1]], axis=0
            )

    wait_bytes(zall.at[pl.ds(0, G - 1)], zr_sem.at[1])
    z_out[...] = zall[...].reshape(G * CH, TILE)
    wait_bytes(zall.at[0, pl.ds(0, G - 1)], zs_sem.at[0])
    wait_bytes(zall.at[pl.ds(0, G - 1)], zs_sem.at[1])
    for it in range(ITERS):
        srows = SUB if it == 0 else SUB + 2
        crows = NB if it + 1 == ITERS else NB + 1
        wait_bytes(gsend.at[it, pl.ds(0, G - 1), pl.ds(0, srows)], send_sem.at[it, 0])
        wait_bytes(rx.at[it, pl.ds(0, G - 1)], send_sem.at[it, 1])
        wait_bytes(sx.at[it, pl.ds(0, G - 1), pl.ds(0, srows)], send_sem.at[it, 2])
        wait_bytes(ez.at[it, pl.ds(0, G - 1)], send_sem.at[it, 3])
        wait_bytes(cx.at[it, pl.ds(0, G - 1), pl.ds(0, crows)], send_sem.at[it, 4])


def local(
    tiles, tile_rows, tile_cols, rhs, coupling, asset, cost_x, upper, cost_z, x_init, z_init, y_init
):
    block = lambda a: a.reshape(NB, TILE)
    inside, anywhere = pl.BlockSpec(memory_space=pltpu.VMEM), pl.BlockSpec(memory_space=pl.ANY)
    x, z, y = pl.pallas_call(
        kernel,
        out_shape=(
            jax.ShapeDtypeStruct((NB, TILE), F32),
            jax.ShapeDtypeStruct((G * CH, TILE), F32),
            jax.ShapeDtypeStruct((NB, TILE), F32),
        ),
        in_specs=[anywhere] + [inside] * 7 + [anywhere, inside, anywhere, inside],
        out_specs=(inside, inside, inside),
        scratch_shapes=[
            pltpu.VMEM((TILES, TILE, TILE), F32),
            pltpu.VMEM((TILES, TILE, 2 * TILE), BF16),
            pltpu.VMEM((TILES, TILE, 2 * TILE), BF16),
            pltpu.VMEM((SUB, TILE), F32),
            pltpu.VMEM((SUB, TILE), F32),
            pltpu.VMEM((NB, TILE), F32),
            pltpu.VMEM((NB, TILE), F32),
            pltpu.VMEM((NB, TILE), F32),
            pltpu.VMEM((NB, TILE), F32),
            pltpu.VMEM((NB, 2 * TILE), F32),
            pltpu.VMEM((NB, TILE), I32),
            pltpu.SMEM((NB, TILE), I32),
            pltpu.VMEM((CH, NB * TILE), BF16),
            pltpu.VMEM((2 * TILE, NB * TILE), BF16),
            pltpu.VMEM((2 * CH, NB * TILE), BF16),
            pltpu.VMEM((ITERS, G, SUB + 2, TILE), F32),
            pltpu.VMEM((ITERS, G, SUB + 2, TILE), F32),
            pltpu.VMEM((ITERS, G, NB, TILE), F32),
            pltpu.VMEM((ITERS, G, SUB + 2, TILE), F32),
            pltpu.VMEM((ITERS, G, SUB, TILE), F32),
            pltpu.VMEM((ITERS, G, NB + 1, TILE), F32),
            pltpu.VMEM((G, G, SUB, TILE), F32),
            pltpu.SemaphoreType.DMA((3,)),
            pltpu.SemaphoreType.DMA,
            pltpu.SemaphoreType.DMA((ITERS, 5)),
            pltpu.SemaphoreType.DMA((ITERS, 5)),
            pltpu.SemaphoreType.DMA((2,)),
            pltpu.SemaphoreType.DMA((2,)),
        ],
        compiler_params=pltpu.CompilerParams(
            collective_id=0, has_side_effects=True, vmem_limit_bytes=32 * 1024 * 1024
        ),
    )(
        tiles.reshape(TILES, TILE, TILE),
        tile_rows.reshape(1, TILES),
        tile_cols.reshape(1, TILES),
        block(rhs),
        block(coupling),
        block(asset),
        block(cost_x),
        block(upper),
        cost_z.reshape(G * CH, TILE),
        block(x_init),
        z_init.reshape(G * CH, TILE),
        block(y_init),
    )
    return x.reshape(1, -1), z.reshape(-1), y.reshape(1, -1)


def solution(mesh):
    in_specs = (
        P("season", "row", "col", None, None, None),
        P("season", "row", "col", None),
        P("season", "row", "col", None),
        P("season", "row"),
        P("season", "row"),
        P("season", "row"),
        P("season", "col"),
        P("season", "col"),
        P(),
        P("season", "col"),
        P(),
        P("season", "row"),
    )
    out_specs = (P("season", "col"), P(), P("season", "row"))
    return jax.shard_map(local, mesh=mesh, in_specs=in_specs, out_specs=out_specs, check_vma=False)
```

time: 2390 us -> 85.5 us (0.04); the launches traced: 2360 us -> 84.9 us
  waiting for transfers between devices: 1500 us -> 0 us
  blocking collectives: 749 us -> 0 us
  Pallas kernels: 0 us -> 72.7 us
  other arithmetic: 45.9 us -> 0 us
    psum x3 -> x0, waiting for transfers between devices: 1500 us -> none  [local(): lax.psum(jax.ops.segment_sum(couple * duals, assets, num_segments=n_inv),...]
    psum x10 -> x0, blocking collectives: 749 us -> none  [the longest x2 338 us: local(): primal_sq = lax.psum(primal_local, ('season', 'col')) + invest_sq]
    pallas_call x0 -> x1, Pallas kernels: none -> 72.7 us  [local(): pl.pallas_call(kernel, out_shape=(jax.ShapeDtypeStruct((NB, TILE), F32),...]
    scatter-add x3 -> x0, other arithmetic: 36.2 us -> none  [local(): jax.ops.segment_sum(couple * duals, assets, num_segments=n_inv)]
    gather x3 -> x0, local copies, waits for them, and re-layouts: 35.3 us -> none  [local(): linked = couple * extra_z[assets]]
  transfers between devices with their start and end apart: 3 -> 0, of which waited for: 3 -> 0; matrix products, arithmetic and copies ran while one was open for 1% -> 0% of each run, Pallas kernels for 0% -> 0%
where the time goes in v1:
time: 85.5 us; the launch traced here: 84.9 us
  Pallas kernels  72.7 us (85%)
  local copies, waits for them, and re-layouts  11.6 us (14%)
    pallas_call x1, Pallas kernels, local(): pl.pallas_call(kernel, out_shape=(jax.ShapeDtypeStruct((NB, TILE), F32),...  72.7 us
    unnamed x27, local copies, waits for them, and re-layouts  11.6 us

profile of v1, /device:TPU:1, one launch (start us, length us, event | category | flops | bytes accessed | tf_op | source)
XLA Modules:
  0.0 84.9 jit_solution(9709661210794821223)
XLA Ops:
  0.6 0.0 copy-start
  0.6 1.6 %copy-done = f32[1,1,1,32,128,128]{5,4,3,2,1,0:T(8,128)S(1)} copy-done((f32[1,1,1,32,128,128]{5,4,3,2,1,0:T(8,128)S(1)}, f32[1,1,1,32,128,128]{5,4,3,2,1,0:T(8,128)}, u32[]{:S(2)}) %copy-start) | copy-done | bytes 2097176
  2.2 0.0 copy-start.1
  2.2 0.9 %copy-done.1 = f32[65536]{0:T(1024)S(1)} copy-done((f32[65536]{0:T(1024)S(1)}, f32[65536]{0:T(1024)}, u32[]{:S(2)}) %copy-start.1) | copy-done | bytes 262168
  3.2 0.0 copy-start.2
  3.2 0.9 %copy-done.2 = f32[65536]{0:T(1024)S(1)} copy-done((f32[65536]{0:T(1024)S(1)}, f32[65536]{0:T(1024)}, u32[]{:S(2)}) %copy-start.2) | copy-done | bytes 262168
  4.1 0.0 copy-start.3
  4.1 0.7 copy-done.3
  4.8 0.0 copy-start.4
  4.8 0.7 copy-done.4
  5.5 0.0 copy-start.5
  5.5 0.7 copy-done.5
  6.2 0.0 copy-start.6
  6.2 0.7 copy-done.6
  6.9 0.0 copy-start.7
  6.9 0.7 copy-done.7
  7.6 0.7 copy-done.8
  8.3 0.7 copy-done.9
  9.0 0.7 copy-done.10
  9.7 0.7 copy-done.11
  10.3 72.7 %shard_map.139 = (f32[16,128]{1,0:T(8,128)S(1)}, f32[512,128]{1,0:T(8,128)S(1)}, f32[16,128]{1,0:T(8,128)S(1)}) custom-call(f32[32,128,128]{2,1,0:T(8,128)S(1)} %bitcast.15, s32[1,32]{1,0:T(1,128)S(1)} %bitcast.28, s32[1,32]{1,0:T(1,128)S(1)} %bitcast.29, f32[16,128]{1,0:T(8,128)S(1)} %bitcast.19, f32[16,128]{1,0:T(8,128)S(1)} %bitcast.20, ...), custom_call_target="tpu_custom_call" | custom-call | tf_op jit(solution)/shard_map/pallas_call | solution.py:298
  83.0 0.6 copy.18
  83.6 0.7 copy.19
  84.3 0.6 copy.20
  (4 shorter events, 0.0 us)
Async XLA Ops:
  0.6 1.6 %copy-start = (f32[1,1,1,32,128,128]{5,4,3,2,1,0:T(8,128)S(1)}, f32[1,1,1,32,128,128]{5,4,3,2,1,0:T(8,128)}, u32[]{:S(2)}) copy-start(f32[1,1,1,32,128,128]{5,4,3,2,1,0:T(8,128)} %param.12) | copy-start | bytes 6291460
  2.2 0.9 %copy-start.1 = (f32[65536]{0:T(1024)S(1)}, f32[65536]{0:T(1024)}, u32[]{:S(2)}) copy-start(f32[65536]{0:T(1024)} %param.20) | copy-start | bytes 786436
  3.2 0.9 %copy-start.2 = (f32[65536]{0:T(1024)S(1)}, f32[65536]{0:T(1024)}, u32[]{:S(2)}) copy-start(f32[65536]{0:T(1024)} %param.22) | copy-start | bytes 786436
  4.1 0.7 copy-start.3
  4.8 0.7 copy-start.4
  5.5 0.7 copy-start.5
  6.2 0.7 copy-start.6
  6.9 0.7 copy-start.7
  7.6 0.7 copy-start.8
  8.3 0.7 copy-start.9
  9.0 0.7 copy-start.10
  9.7 0.7 copy-start.11

commit v2 on v1

--- a/solution.py
+++ b/solution.py
@@ -10,6 +10,7 @@
 ITERS = 3
 STEP_SCALE = 0.35
 EPSILON = 1e-06
+VMEM_LIMIT = 32 * 1024 * 1024
 
 MESH = pl.DeviceIdType.MESH
 F32, BF16, I32 = jnp.float32, jnp.bfloat16, jnp.int32
@@ -19,15 +20,26 @@
 TILES = 32
 CH = 64
 SUB = CH // G
-
-
-def peer(axis, k):
-    return {axis: lax.rem(lax.axis_index(axis) + k, G)}
+HALF = pl.ds(0, SUB // 2), pl.ds(SUB // 2, SUB // 2)
+
+
+NEAR = {"season": 8, "row": 4, "col": 2}
+FAR_FIRST = {
+    "season": [(0, 4), (0, 3), (0, 5), (0, 2), (0, 6), (0, 1), (0, 7)],
+    "row": [(1, 2), (0, 2), (1, 1), (1, 3), (0, 1), (0, 3), (1, 0)],
+    "col": [(2, 0), (2, 1), (1, 0), (3, 0), (1, 1), (3, 1), (0, 1)],
+}
+
+
+def others(axis):
+    me, n = lax.axis_index(axis), NEAR[axis]
+    i, j = me // n, lax.rem(me, n)
+    return [lax.rem(i + a, G // n) * n + lax.rem(j + b, n) for a, b in FAR_FIRST[axis]]
 
 
 def to_peers(axis, copy):
-    for k in range(1, G):
-        copy(lax.rem(lax.axis_index(axis) + k, G), peer(axis, k))
+    for to in others(axis):
+        copy(to, {axis: to})
 
 
 def wait_bytes(ref, sem):
@@ -64,35 +76,31 @@
 
 
 def kernel(
-    tiles_hbm, rows_ref, cols_ref, rhs_ref, coup_ref, asset_ref, costx_ref, upper_ref, costz_hbm, x0_ref, z0_hbm, y0_ref,
+    tiles_hbm, rows_hbm, cols_hbm, rhs_hbm, coup_hbm, asset_hbm, costx_hbm, upper_hbm, costz_hbm, x0_hbm, z0_hbm, y0_hbm,
     x_out, z_out, y_out,
-    tiles, tb, tf, costz, zv, xv, yv, tr, fw, picked, order_v, order, hot_hi, hot_lo, left,
-    gsend, rs, rx, sx, ez, cx, zall,
+    tiles, rows_ref, cols_ref, rhs_ref, coup_ref, asset_ref, costx_ref, upper_ref, costz, xv, zv, yv,
+    tb, tf, tr, fw, picked, order_v, order, mask, hot_hi, hot_lo, left,
+    gsend, rs, rx, sx, ez, cx,
     load_sem, order_sem, send_sem, recv_sem, zs_sem, zr_sem,
 ):
     s, r, c = (lax.axis_index(a) for a in ("season", "row", "col"))
     barrier = pltpu.get_barrier_semaphore()
     for axis in ("season", "row", "col"):
-        for k in range(1, G):
-            pl.semaphore_signal(barrier, inc=1, device_id=peer(axis, k), device_id_type=MESH)
+        for to in others(axis):
+            pl.semaphore_signal(barrier, inc=1, device_id={axis: to}, device_id_type=MESH)
     mine = pl.ds(pl.multiple_of(c * CH + r * SUB, SUB), SUB)
     loads = [
-        pltpu.make_async_copy(costz_hbm.at[mine], costz, load_sem.at[0]),
-        pltpu.make_async_copy(z0_hbm.at[mine], zv, load_sem.at[1]),
-        pltpu.make_async_copy(tiles_hbm, tiles, load_sem.at[2]),
+        pltpu.make_async_copy(there, here, load_sem.at[k])
+        for k, (there, here) in enumerate([
+            (asset_hbm, asset_ref), (coup_hbm, coup_ref), (y0_hbm, yv), (rows_hbm, rows_ref), (cols_hbm, cols_ref),
+            (tiles_hbm, tiles), (costz_hbm.at[mine], costz), (z0_hbm.at[mine], zv), (x0_hbm, xv),
+            (costx_hbm, costx_ref), (upper_hbm, upper_ref), (rhs_hbm, rhs_ref),
+        ])
     ]
     for load in loads:
         load.start()
 
-    rows, cols = rows_ref[...], cols_ref[...]
-    place = lax.broadcasted_iota(I32, (NB, TILE), 1)
-    table = jnp.zeros((NB, TILE), I32)
-    for at, col in enumerate(first_and_last(cols, rows) + first_and_last(rows, cols)):
-        table = jnp.where(place == at, col, table)
-    order_v[...] = table
-    to_smem = pltpu.make_async_copy(order_v, order, order_sem)
-    to_smem.start()
-
+    loads[0].wait()
     asset = asset_ref[...]
     low, high = asset & (TILE - 1), (asset >> 7) - c * CH
     for n in range(NB):
@@ -102,11 +110,23 @@
         hot_lo[0:TILE, at] = one
         hot_lo[TILE : 2 * TILE, at] = one
         hit = lax.broadcasted_iota(I32, (CH, TILE), 0) == high[n : n + 1, :]
-        hot_hi[:, at] = jnp.where(hit, 1.0, 0.0).astype(BF16)
-
+        one = jnp.where(hit, 1.0, 0.0)
+        mask[:, at] = one
+        hot_hi[:, at] = one.astype(BF16)
+
+    loads[1].wait()
+    loads[2].wait()
     coup = coup_ref[...]
-    xv[...] = x0_ref[...]
-    yv[...] = y0_ref[...]
+
+    def send_z(k, axis, blocks):
+        def send(to, device):
+            pltpu.make_async_remote_copy(
+                src_ref=blocks, dst_ref=blocks,
+                send_sem=zs_sem.at[k], recv_sem=zr_sem.at[k], device_id=device, device_id_type=MESH,
+            ).start()
+
+        to_peers(axis, send)
+
     balance = None
     stats = None
     for it in range(ITERS):
@@ -143,12 +163,22 @@
         rs[it, r] = gsend[it, r]
 
         if it == 0:
-            to_smem.wait()
-            loads[2].wait()
+            loads[3].wait()
+            loads[4].wait()
+            rows, cols = rows_ref[...], cols_ref[...]
+            place = lax.broadcasted_iota(I32, (NB, TILE), 1)
+            table = jnp.zeros((NB, TILE), I32)
+            for at, col in enumerate(first_and_last(cols, rows) + first_and_last(rows, cols)):
+                table = jnp.where(place == at, col, table)
+            order_v[...] = table
+            to_smem = pltpu.make_async_copy(order_v, order, order_sem)
+            to_smem.start()
+            loads[5].wait()
             for k in range(TILES):
                 t_high, t_low = split2(tiles[k])
                 tb[k, :, 0:TILE] = t_high
                 tb[k, :, TILE : 2 * TILE] = t_low
+            to_smem.wait()
 
         def put(b, row):
             rx[it, r, b : b + 1, :] = row
@@ -180,8 +210,8 @@
                 t_high, t_low = split2(tiles[k].T)
                 tf[k, :, 0:TILE] = t_high
                 tf[k, :, TILE : 2 * TILE] = t_low
-            loads[0].wait()
-            loads[1].wait()
+            for load in loads[6:]:
+                load.wait()
         wait_bytes(rx.at[it, pl.ds(0, G - 1)], x_recvs)
         transposed = jnp.sum(rx[it], axis=0)
         wait_bytes(sx.at[it, pl.ds(0, G - 1), pl.ds(0, srows)], recvs)
@@ -191,9 +221,11 @@
         else:
             dual_sq = jnp.sum(total[SUB : SUB + 1], axis=1, keepdims=True)
             primal_sq = jnp.sum(total[SUB + 1 : SUB + 2], axis=1, keepdims=True) * (1.0 / G)
-            root = jnp.sqrt((primal_sq + EPSILON) / (dual_sq + EPSILON))
-            balance = jnp.sqrt(root if balance is None else balance * root)
-            primal_step, dual_step = STEP_SCALE / balance, STEP_SCALE * balance
+            square = jnp.sqrt(primal_sq + EPSILON) * lax.rsqrt(dual_sq + EPSILON)
+            if balance is not None:
+                square = balance * square
+            balance = jnp.sqrt(square)
+            primal_step, dual_step = STEP_SCALE * lax.rsqrt(square), STEP_SCALE * balance
 
         z_old = zv[...]
         z_new = jnp.maximum(z_old - primal_step * (costz[...] - total[0:SUB]), 0.0)
@@ -209,15 +241,9 @@
 
         to_peers("row", send)
         if last:
-            zall[c, r] = z_new
-
-            def send(to, device):
-                pltpu.make_async_remote_copy(
-                    src_ref=zall.at[c, r], dst_ref=zall.at[c, r],
-                    send_sem=zs_sem.at[0], recv_sem=zr_sem.at[0], device_id=device, device_id_type=MESH,
-                ).start()
-
-            to_peers("row", send)
+            z_out[c, r] = z_new
+            send_z(0, "row", z_out.at[c, r, HALF[0]])
+            send_z(2, "col", z_out.at[c, r, HALF[1]])
 
         x_old = xv[...]
         x_new = jnp.clip(x_old - primal_step * (costx_ref[...] - transposed), 0.0, upper_ref[...])
@@ -230,7 +256,6 @@
         products(order, 4, tf, tr, picked, put)
         if last:
             x_out[...] = x_new
-            wait_bytes(zall.at[0, pl.ds(0, G - 1)], zr_sem.at[0])
         else:
             cx[it, c, NB : NB + 1] = jnp.sum((x_new - x_old) ** 2, axis=0, keepdims=True) + jnp.sum(
                 (z_new - z_old) ** 2, axis=0, keepdims=True
@@ -243,7 +268,7 @@
         )
         for n in range(NB):
             at = slice(n * TILE, (n + 1) * TILE)
-            linked = jnp.sum(gathered[:, at] * hot_hi[:, at].astype(F32), axis=0, keepdims=True)
+            linked = jnp.sum(gathered[:, at] * mask[:, at], axis=0, keepdims=True)
             cx[it, c, n : n + 1] = fw[n : n + 1, :] + coup[n : n + 1, :] * linked
         sends, recvs = sem(4)
 
@@ -255,14 +280,10 @@
 
         to_peers("col", send)
         if last:
-
-            def send(to, device):
-                pltpu.make_async_remote_copy(
-                    src_ref=zall.at[c], dst_ref=zall.at[c],
-                    send_sem=zs_sem.at[1], recv_sem=zr_sem.at[1], device_id=device, device_id_type=MESH,
-                ).start()
-
-            to_peers("col", send)
+            wait_bytes(z_out.at[0, pl.ds(0, G - 1), HALF[0]], zr_sem.at[0])
+            send_z(1, "col", z_out.at[c, :, HALF[0]])
+            wait_bytes(z_out.at[pl.ds(0, G - 1), 0, HALF[1]], zr_sem.at[2])
+            send_z(3, "row", z_out.at[:, r, HALF[1]])
         wait_bytes(cx.at[it, pl.ds(0, G - 1), pl.ds(0, crows)], recvs)
         image = jnp.sum(cx[it, :, 0:crows], axis=0)
 
@@ -276,10 +297,11 @@
                 [jnp.sum((y_new - y_old) ** 2, axis=0, keepdims=True), image[NB : NB + 1]], axis=0
             )
 
-    wait_bytes(zall.at[pl.ds(0, G - 1)], zr_sem.at[1])
-    z_out[...] = zall[...].reshape(G * CH, TILE)
-    wait_bytes(zall.at[0, pl.ds(0, G - 1)], zs_sem.at[0])
-    wait_bytes(zall.at[pl.ds(0, G - 1)], zs_sem.at[1])
+    for half in range(2):
+        step, blocks = HALF[half], pl.ds(0, G - 1)
+        wait_bytes(z_out.at[blocks, :, step], zr_sem.at[2 * half + 1])
+        wait_bytes(z_out.at[0, blocks, step], zs_sem.at[2 * half])
+        wait_bytes(z_out.at[blocks, :, step], zs_sem.at[2 * half + 1])
     for it in range(ITERS):
         srows = SUB if it == 0 else SUB + 2
         crows = NB if it + 1 == ITERS else NB + 1
@@ -290,54 +312,25 @@
         wait_bytes(cx.at[it, pl.ds(0, G - 1), pl.ds(0, crows)], send_sem.at[it, 4])
 
 
+def place(x_ref, z_ref, y_ref, x_out, z_out, y_out, sem):
+    copies = [
+        pltpu.make_async_copy(here, there, sem.at[k])
+        for k, (here, there) in enumerate([(z_ref, z_out), (x_ref, x_out), (y_ref, y_out)])
+    ]
+    for copy in copies:
+        copy.start()
+    for copy in copies:
+        copy.wait()
+
+
 def local(
     tiles, tile_rows, tile_cols, rhs, coupling, asset, cost_x, upper, cost_z, x_init, z_init, y_init
 ):
     block = lambda a: a.reshape(NB, TILE)
-    inside, anywhere = pl.BlockSpec(memory_space=pltpu.VMEM), pl.BlockSpec(memory_space=pl.ANY)
-    x, z, y = pl.pallas_call(
-        kernel,
-        out_shape=(
-            jax.ShapeDtypeStruct((NB, TILE), F32),
-            jax.ShapeDtypeStruct((G * CH, TILE), F32),
-            jax.ShapeDtypeStruct((NB, TILE), F32),
-        ),
-        in_specs=[anywhere] + [inside] * 7 + [anywhere, inside, anywhere, inside],
-        out_specs=(inside, inside, inside),
-        scratch_shapes=[
-            pltpu.VMEM((TILES, TILE, TILE), F32),
-            pltpu.VMEM((TILES, TILE, 2 * TILE), BF16),
-            pltpu.VMEM((TILES, TILE, 2 * TILE), BF16),
-            pltpu.VMEM((SUB, TILE), F32),
-            pltpu.VMEM((SUB, TILE), F32),
-            pltpu.VMEM((NB, TILE), F32),
-            pltpu.VMEM((NB, TILE), F32),
-            pltpu.VMEM((NB, TILE), F32),
-            pltpu.VMEM((NB, TILE), F32),
-            pltpu.VMEM((NB, 2 * TILE), F32),
-            pltpu.VMEM((NB, TILE), I32),
-            pltpu.SMEM((NB, TILE), I32),
-            pltpu.VMEM((CH, NB * TILE), BF16),
-            pltpu.VMEM((2 * TILE, NB * TILE), BF16),
-            pltpu.VMEM((2 * CH, NB * TILE), BF16),
-            pltpu.VMEM((ITERS, G, SUB + 2, TILE), F32),
-            pltpu.VMEM((ITERS, G, SUB + 2, TILE), F32),
-            pltpu.VMEM((ITERS, G, NB, TILE), F32),
-            pltpu.VMEM((ITERS, G, SUB + 2, TILE), F32),
-            pltpu.VMEM((ITERS, G, SUB, TILE), F32),
-            pltpu.VMEM((ITERS, G, NB + 1, TILE), F32),
-            pltpu.VMEM((G, G, SUB, TILE), F32),
-            pltpu.SemaphoreType.DMA((3,)),
-            pltpu.SemaphoreType.DMA,
-            pltpu.SemaphoreType.DMA((ITERS, 5)),
-            pltpu.SemaphoreType.DMA((ITERS, 5)),
-            pltpu.SemaphoreType.DMA((2,)),
-            pltpu.SemaphoreType.DMA((2,)),
-        ],
-        compiler_params=pltpu.CompilerParams(
-            collective_id=0, has_side_effects=True, vmem_limit_bytes=32 * 1024 * 1024
-        ),
-    )(
+    inside = pl.BlockSpec(memory_space=pltpu.VMEM)
+    in_hbm = lambda a: pltpu.with_memory_space_constraint(a, pltpu.HBM)
+    in_vmem = lambda a: pltpu.with_memory_space_constraint(a, pltpu.VMEM)
+    operands = (
         tiles.reshape(TILES, TILE, TILE),
         tile_rows.reshape(1, TILES),
         tile_cols.reshape(1, TILES),
@@ -351,6 +344,61 @@
         z_init.reshape(G * CH, TILE),
         block(y_init),
     )
+    x, z, y = pl.pallas_call(
+        kernel,
+        out_shape=(
+            pltpu.VMEM((NB, TILE), F32), pltpu.VMEM((G, G, SUB, TILE), F32), pltpu.VMEM((NB, TILE), F32),
+        ),
+        in_specs=[pl.BlockSpec(memory_space=pltpu.HBM)] * 12,
+        out_specs=(inside, inside, inside),
+        scratch_shapes=[
+            pltpu.VMEM((TILES, TILE, TILE), F32),
+            pltpu.VMEM((1, TILES), I32),
+            pltpu.VMEM((1, TILES), I32),
+            pltpu.VMEM((NB, TILE), F32),
+            pltpu.VMEM((NB, TILE), F32),
+            pltpu.VMEM((NB, TILE), I32),
+            pltpu.VMEM((NB, TILE), F32),
+            pltpu.VMEM((NB, TILE), F32),
+            pltpu.VMEM((SUB, TILE), F32),
+            pltpu.VMEM((NB, TILE), F32),
+            pltpu.VMEM((SUB, TILE), F32),
+            pltpu.VMEM((NB, TILE), F32),
+            pltpu.VMEM((TILES, TILE, 2 * TILE), BF16),
+            pltpu.VMEM((TILES, TILE, 2 * TILE), BF16),
+            pltpu.VMEM((NB, TILE), F32),
+            pltpu.VMEM((NB, TILE), F32),
+            pltpu.VMEM((NB, 2 * TILE), F32),
+            pltpu.VMEM((NB, TILE), I32),
+            pltpu.SMEM((NB, TILE), I32),
+            pltpu.VMEM((CH, NB * TILE), F32),
+            pltpu.VMEM((CH, NB * TILE), BF16),
+            pltpu.VMEM((2 * TILE, NB * TILE), BF16),
+            pltpu.VMEM((2 * CH, NB * TILE), BF16),
+            pltpu.VMEM((ITERS, G, SUB + 2, TILE), F32),
+            pltpu.VMEM((ITERS, G, SUB + 2, TILE), F32),
+            pltpu.VMEM((ITERS, G, NB, TILE), F32),
+            pltpu.VMEM((ITERS, G, SUB + 2, TILE), F32),
+            pltpu.VMEM((ITERS, G, SUB, TILE), F32),
+            pltpu.VMEM((ITERS, G, NB + 1, TILE), F32),
+            pltpu.SemaphoreType.DMA((12,)),
+            pltpu.SemaphoreType.DMA,
+            pltpu.SemaphoreType.DMA((ITERS, 5)),
+            pltpu.SemaphoreType.DMA((ITERS, 5)),
+            pltpu.SemaphoreType.DMA((4,)),
+            pltpu.SemaphoreType.DMA((4,)),
+        ],
+        compiler_params=pltpu.CompilerParams(
+            collective_id=0, has_side_effects=True, vmem_limit_bytes=VMEM_LIMIT
+        ),
+    )(*map(in_hbm, operands))
+    x, z, y = pl.pallas_call(
+        place,
+        out_shape=tuple(jax.ShapeDtypeStruct(a.shape, F32) for a in (x, z, y)),
+        in_specs=[inside] * 3,
+        out_specs=(pl.BlockSpec(memory_space=pl.ANY),) * 3,
+        scratch_shapes=[pltpu.SemaphoreType.DMA((3,))],
+    )(*map(in_vmem, (x, z, y)))
     return x.reshape(1, -1), z.reshape(-1), y.reshape(1, -1)
 
 

time: 85.5 us -> 72.1 us (0.84)
  local copies, waits for them, and re-layouts: 11.6 us -> 0 us
  Pallas kernels: 72.7 us -> 71.3 us
    unnamed x27 -> x0, local copies, waits for them, and re-layouts: 11.6 us -> none
    pallas_call x1 -> x2, Pallas kernels: 72.7 us -> 71.3 us  [the longest x1 70.6 us: local(): pl.pallas_call(kernel, out_shape=(pltpu.VMEM((NB, TILE), F32), pltpu.VMEM...]
where the time goes in v2:
time: 72.1 us; the launch traced here: 71.9 us
  Pallas kernels  71.3 us (99%)
    pallas_call x1, Pallas kernels, local(): pl.pallas_call(kernel, out_shape=(pltpu.VMEM((NB, TILE), F32), pltpu.VMEM...  70.6 us

profile of v2, /device:TPU:1, one launch (start us, length us, event | category | flops | bytes accessed | tf_op | source)
XLA Modules:
  0.0 71.9 jit_solution(5930201795080971988)
XLA Ops:
  0.6 70.6 %shard_map.139 = (f32[16,128]{1,0:T(8,128)S(1)}, f32[8,8,8,128]{3,2,1,0:T(8,128)S(1)}, f32[16,128]{1,0:T(8,128)S(1)}) custom-call(f32[32,128,128]{2,1,0:T(8,128)} %bitcast.15, s32[1,32]{1,0:T(1,128)} %bitcast.25, s32[1,32]{1,0:T(1,128)} %bitcast.26, f32[16,128]{1,0:T(8,128)} %bitcast.18, f32[16,128]{1,0:T(8,128)} %bitcast.19, s32[16,128]{1,0:T(8,128)} %bitcast.20, ...), custom_call_target="tpu_custom_call" | custom-call | tf_op jit(solution)/shard_map/pallas_call | solution.py:347
  71.2 0.7 %shard_map.140 = (f32[16,128]{1,0:T(8,128)}, f32[8,8,8,128]{3,2,1,0:T(8,128)}, f32[16,128]{1,0:T(8,128)}) custom-call(f32[16,128]{1,0:T(8,128)S(1)} %get-tuple-element.9.x_ref, f32[8,8,8,128]{3,2,1,0:T(8,128)S(1)} %get-tuple-element.10.z_ref, f32[16,128]{1,0:T(8,128)S(1)} %get-tuple-element.11.y_ref), custom_call_target="tpu_custom_call" | custom-call | tf_op jit(solution)/shard_map/pallas_call | solution.py:395

commit v3 on v2

--- a/solution.py
+++ b/solution.py
@@ -20,7 +20,7 @@
 TILES = 32
 CH = 64
 SUB = CH // G
-HALF = pl.ds(0, SUB // 2), pl.ds(SUB // 2, SUB // 2)
+STRAIGHT, TWO_STEPS = pl.ds(0, 3), pl.ds(3, SUB - 3)
 
 
 NEAR = {"season": 8, "row": 4, "col": 2}
@@ -80,7 +80,7 @@
     x_out, z_out, y_out,
     tiles, rows_ref, cols_ref, rhs_ref, coup_ref, asset_ref, costx_ref, upper_ref, costz, xv, zv, yv,
     tb, tf, tr, fw, picked, order_v, order, mask, hot_hi, hot_lo, left,
-    gsend, rs, rx, sx, ez, cx,
+    gsend, rs, rx, sx, ez, cx, rows_in,
     load_sem, order_sem, send_sem, recv_sem, zs_sem, zr_sem,
 ):
     s, r, c = (lax.axis_index(a) for a in ("season", "row", "col"))
@@ -242,8 +242,7 @@
         to_peers("row", send)
         if last:
             z_out[c, r] = z_new
-            send_z(0, "row", z_out.at[c, r, HALF[0]])
-            send_z(2, "col", z_out.at[c, r, HALF[1]])
+            send_z(0, "col", z_out.at[c, r, TWO_STEPS])
 
         x_old = xv[...]
         x_new = jnp.clip(x_old - primal_step * (costx_ref[...] - transposed), 0.0, upper_ref[...])
@@ -256,6 +255,14 @@
         products(order, 4, tf, tr, picked, put)
         if last:
             x_out[...] = x_new
+            for to_c in [c] + others("col"):
+                for to_r in [r] + others("row"):
+                    if to_c is not c or to_r is not r:
+                        pltpu.make_async_remote_copy(
+                            src_ref=z_out.at[c, r, STRAIGHT], dst_ref=z_out.at[c, r, STRAIGHT],
+                            send_sem=zs_sem.at[2], recv_sem=zr_sem.at[2],
+                            device_id={"row": to_r, "col": to_c}, device_id_type=MESH,
+                        ).start()
         else:
             cx[it, c, NB : NB + 1] = jnp.sum((x_new - x_old) ** 2, axis=0, keepdims=True) + jnp.sum(
                 (z_new - z_old) ** 2, axis=0, keepdims=True
@@ -280,10 +287,8 @@
 
         to_peers("col", send)
         if last:
-            wait_bytes(z_out.at[0, pl.ds(0, G - 1), HALF[0]], zr_sem.at[0])
-            send_z(1, "col", z_out.at[c, :, HALF[0]])
-            wait_bytes(z_out.at[pl.ds(0, G - 1), 0, HALF[1]], zr_sem.at[2])
-            send_z(3, "row", z_out.at[:, r, HALF[1]])
+            wait_bytes(z_out.at[pl.ds(0, G - 1), 0, TWO_STEPS], zr_sem.at[0])
+            send_z(1, "row", z_out.at[:, r, TWO_STEPS])
         wait_bytes(cx.at[it, pl.ds(0, G - 1), pl.ds(0, crows)], recvs)
         image = jnp.sum(cx[it, :, 0:crows], axis=0)
 
@@ -297,11 +302,11 @@
                 [jnp.sum((y_new - y_old) ** 2, axis=0, keepdims=True), image[NB : NB + 1]], axis=0
             )
 
-    for half in range(2):
-        step, blocks = HALF[half], pl.ds(0, G - 1)
-        wait_bytes(z_out.at[blocks, :, step], zr_sem.at[2 * half + 1])
-        wait_bytes(z_out.at[0, blocks, step], zs_sem.at[2 * half])
-        wait_bytes(z_out.at[blocks, :, step], zs_sem.at[2 * half + 1])
+    wait_bytes(z_out.at[pl.ds(0, G - 1), :, TWO_STEPS], zr_sem.at[1])
+    wait_bytes(z_out.at[pl.ds(0, G - 1), 0, TWO_STEPS], zs_sem.at[0])
+    wait_bytes(z_out.at[pl.ds(0, G - 1), :, TWO_STEPS], zs_sem.at[1])
+    for sem in (zr_sem.at[2], zs_sem.at[2]):
+        wait_bytes(rows_in.at[pl.ds(0, 3 * (G * G - 1))], sem)
     for it in range(ITERS):
         srows = SUB if it == 0 else SUB + 2
         crows = NB if it + 1 == ITERS else NB + 1
@@ -381,12 +386,13 @@
             pltpu.VMEM((ITERS, G, SUB + 2, TILE), F32),
             pltpu.VMEM((ITERS, G, SUB, TILE), F32),
             pltpu.VMEM((ITERS, G, NB + 1, TILE), F32),
+            pltpu.VMEM((3 * G * G, TILE), F32),
             pltpu.SemaphoreType.DMA((12,)),
             pltpu.SemaphoreType.DMA,
             pltpu.SemaphoreType.DMA((ITERS, 5)),
             pltpu.SemaphoreType.DMA((ITERS, 5)),
-            pltpu.SemaphoreType.DMA((4,)),
-            pltpu.SemaphoreType.DMA((4,)),
+            pltpu.SemaphoreType.DMA((3,)),
+            pltpu.SemaphoreType.DMA((3,)),
         ],
         compiler_params=pltpu.CompilerParams(
             collective_id=0, has_side_effects=True, vmem_limit_bytes=VMEM_LIMIT

time: 72.1 us -> 70.1 us (0.972)
  Pallas kernels: 71.3 us -> 69.3 us
    pallas_call x1, Pallas kernels: 70.6 us -> 68.6 us  [local(): pl.pallas_call(kernel, out_shape=(pltpu.VMEM((NB, TILE), F32), pltpu.VMEM...]
where the time goes in v3:
time: 70.1 us; the launch traced here: 70 us
  Pallas kernels  69.3 us (99%)
    pallas_call x1, Pallas kernels, local(): pl.pallas_call(kernel, out_shape=(pltpu.VMEM((NB, TILE), F32), pltpu.VMEM...  68.6 us

profile of v3, /device:TPU:1, one launch (start us, length us, event | category | flops | bytes accessed | tf_op | source)
XLA Modules:
  0.0 70.0 jit_solution(3770091815657601271)
XLA Ops:
  0.6 68.6 %shard_map.139 = (f32[16,128]{1,0:T(8,128)S(1)}, f32[8,8,8,128]{3,2,1,0:T(8,128)S(1)}, f32[16,128]{1,0:T(8,128)S(1)}) custom-call(f32[32,128,128]{2,1,0:T(8,128)} %bitcast.15, s32[1,32]{1,0:T(1,128)} %bitcast.25, s32[1,32]{1,0:T(1,128)} %bitcast.26, f32[16,128]{1,0:T(8,128)} %bitcast.18, f32[16,128]{1,0:T(8,128)} %bitcast.19, s32[16,128]{1,0:T(8,128)} %bitcast.20, ...), custom_call_target="tpu_custom_call" | custom-call | tf_op jit(solution)/shard_map/pallas_call | solution.py:352
  69.2 0.7 %shard_map.140 = (f32[16,128]{1,0:T(8,128)}, f32[8,8,8,128]{3,2,1,0:T(8,128)}, f32[16,128]{1,0:T(8,128)}) custom-call(f32[16,128]{1,0:T(8,128)S(1)} %get-tuple-element.9.x_ref, f32[8,8,8,128]{3,2,1,0:T(8,128)S(1)} %get-tuple-element.10.z_ref, f32[16,128]{1,0:T(8,128)S(1)} %get-tuple-element.11.y_ref), custom_call_target="tpu_custom_call" | custom-call | tf_op jit(solution)/shard_map/pallas_call | solution.py:401

commit v4 on v3

--- a/solution.py
+++ b/solution.py
@@ -20,6 +20,7 @@
 TILES = 32
 CH = 64
 SUB = CH // G
+EARLY = 4
 STRAIGHT, TWO_STEPS = pl.ds(0, 3), pl.ds(3, SUB - 3)
 
 
@@ -79,22 +80,30 @@
     tiles_hbm, rows_hbm, cols_hbm, rhs_hbm, coup_hbm, asset_hbm, costx_hbm, upper_hbm, costz_hbm, x0_hbm, z0_hbm, y0_hbm,
     x_out, z_out, y_out,
     tiles, rows_ref, cols_ref, rhs_ref, coup_ref, asset_ref, costx_ref, upper_ref, costz, xv, zv, yv,
-    tb, tf, tr, fw, picked, order_v, order, mask, hot_hi, hot_lo, left,
+    costz_pair, z_pair, z_in, tb, tf, tr, fw, picked, order_v, order, mask, hot_hi, hot_lo, left,
     gsend, rs, rx, sx, ez, cx, rows_in,
-    load_sem, order_sem, send_sem, recv_sem, zs_sem, zr_sem,
+    load_sem, order_sem, send_sem, recv_sem, zs_sem, zr_sem, pair_sem, here_sem,
 ):
     s, r, c = (lax.axis_index(a) for a in ("season", "row", "col"))
     barrier = pltpu.get_barrier_semaphore()
-    for axis in ("season", "row", "col"):
+    early, late = c < EARLY, c >= EARLY
+    for axis in ("season", "row"):
         for to in others(axis):
             pl.semaphore_signal(barrier, inc=1, device_id={axis: to}, device_id_type=MESH)
+    for to in others("col"):
+        @pl.when(jnp.logical_or(early, to >= EARLY))
+        def _():
+            pl.semaphore_signal(barrier, inc=1, device_id={"col": to}, device_id_type=MESH)
+
     mine = pl.ds(pl.multiple_of(c * CH + r * SUB, SUB), SUB)
+    pair = pl.ds(pl.multiple_of(lax.rem(c + EARLY, G) * CH + r * SUB, SUB), SUB)
     loads = [
         pltpu.make_async_copy(there, here, load_sem.at[k])
         for k, (there, here) in enumerate([
             (asset_hbm, asset_ref), (coup_hbm, coup_ref), (y0_hbm, yv), (rows_hbm, rows_ref), (cols_hbm, cols_ref),
             (tiles_hbm, tiles), (costz_hbm.at[mine], costz), (z0_hbm.at[mine], zv), (x0_hbm, xv),
             (costx_hbm, costx_ref), (upper_hbm, upper_ref), (rhs_hbm, rhs_ref),
+            (costz_hbm.at[pair], costz_pair), (z0_hbm.at[pair], z_pair),
         ])
     ]
     for load in loads:
@@ -103,6 +112,7 @@
     loads[0].wait()
     asset = asset_ref[...]
     low, high = asset & (TILE - 1), (asset >> 7) - c * CH
+    high_pair = high - EARLY * CH
     for n in range(NB):
         at = slice(n * TILE, (n + 1) * TILE)
         hit = lax.broadcasted_iota(I32, (TILE, TILE), 0) == low[n : n + 1, :]
@@ -111,56 +121,90 @@
         hot_lo[TILE : 2 * TILE, at] = one
         hit = lax.broadcasted_iota(I32, (CH, TILE), 0) == high[n : n + 1, :]
         one = jnp.where(hit, 1.0, 0.0)
-        mask[:, at] = one
-        hot_hi[:, at] = one.astype(BF16)
+        mask[0, :, at] = one
+        hot_hi[0, :, at] = one.astype(BF16)
+
+    @pl.when(early)
+    def _():
+        for n in range(NB):
+            at = slice(n * TILE, (n + 1) * TILE)
+            hit = lax.broadcasted_iota(I32, (CH, TILE), 0) == high_pair[n : n + 1, :]
+            one = jnp.where(hit, 1.0, 0.0)
+            mask[1, :, at] = one
+            hot_hi[1, :, at] = one.astype(BF16)
 
     loads[1].wait()
     loads[2].wait()
     coup = coup_ref[...]
 
+    def spread(axis, blocks, send, recv):
+        def start(to, device):
+            pltpu.make_async_remote_copy(
+                src_ref=blocks, dst_ref=blocks, send_sem=send, recv_sem=recv, device_id=device, device_id_type=MESH
+            ).start()
+
+        to_peers(axis, start)
+
+    def z_to_pair(to):
+        return pltpu.make_async_remote_copy(
+            src_ref=z_pair, dst_ref=z_in, send_sem=pair_sem.at[0], recv_sem=pair_sem.at[1],
+            device_id={"col": to}, device_id_type=MESH,
+        )
+
     def send_z(k, axis, blocks):
-        def send(to, device):
-            pltpu.make_async_remote_copy(
-                src_ref=blocks, dst_ref=blocks,
-                send_sem=zs_sem.at[k], recv_sem=zr_sem.at[k], device_id=device, device_id_type=MESH,
-            ).start()
-
-        to_peers(axis, send)
+        spread(axis, blocks, zs_sem.at[k], zr_sem.at[k])
+
+    def investment(k):
+        v_high, v_low = split2(coup * yv[...])
+        for n in range(NB):
+            at = slice(n * TILE, (n + 1) * TILE)
+            hot = hot_hi[k, :, at]
+            left[k, 0:CH, at] = hot * v_high[n : n + 1, :]
+            left[k, CH : 2 * CH, at] = hot * v_low[n : n + 1, :]
+        cap = lax.dot_general(
+            left[k], hot_lo[0:TILE, :], (((1,), (1,)), ((), ())), preferred_element_type=F32
+        )
+        return cap[0:CH] + cap[CH : 2 * CH]
+
+    def linked(k, values):
+        e_high, e_low = split2(values)
+        gathered = jnp.dot(
+            jnp.concatenate([e_high, e_low], axis=1), hot_lo[...], preferred_element_type=F32
+        )
+        for n in range(NB):
+            at = slice(n * TILE, (n + 1) * TILE)
+            yield n, coup[n : n + 1, :] * jnp.sum(gathered[:, at] * mask[k, :, at], axis=0, keepdims=True)
 
     balance = None
     stats = None
     for it in range(ITERS):
         last = it + 1 == ITERS
-        srows = SUB if it == 0 else SUB + 2
+        srows = 2 * SUB if it == 0 else SUB + 2
         crows = NB if last else NB + 1
         sem = lambda phase: (send_sem.at[it, phase], recv_sem.at[it, phase])
 
-        v_high, v_low = split2(coup * yv[...])
-        for n in range(NB):
-            at = slice(n * TILE, (n + 1) * TILE)
-            hot = hot_hi[:, at]
-            left[0:CH, at] = hot * v_high[n : n + 1, :]
-            left[CH : 2 * CH, at] = hot * v_low[n : n + 1, :]
-        cap = lax.dot_general(
-            left[...], hot_lo[0:TILE, :], (((1,), (1,)), ((), ())), preferred_element_type=F32
-        )
-        cap = cap[0:CH] + cap[CH : 2 * CH]
-        for k in range(G):
-            gsend[it, k, 0:SUB] = cap[k * SUB : (k + 1) * SUB]
-            if it:
-                gsend[it, k, SUB : SUB + 2] = stats
-        if it == 0:
-            pl.semaphore_wait(barrier, 3 * (G - 1))
-        sends, recvs = sem(0)
-
-        def send(to, device):
+        def send_sums(to, device):
             pltpu.make_async_remote_copy(
                 src_ref=gsend.at[it, to, pl.ds(0, srows)], dst_ref=rs.at[it, r, pl.ds(0, srows)],
-                send_sem=sends, recv_sem=recvs, device_id=device, device_id_type=MESH,
+                send_sem=send_sem.at[it, 0], recv_sem=recv_sem.at[it, 0], device_id=device, device_id_type=MESH,
             ).start()
 
-        to_peers("row", send)
-        rs[it, r] = gsend[it, r]
+        if it == 0:
+
+            @pl.when(early)
+            def _():
+                for half in range(2):
+                    cap = investment(half)
+                    for k in range(G):
+                        gsend[0, k, half * SUB : (half + 1) * SUB] = cap[k * SUB : (k + 1) * SUB]
+
+        else:
+            cap = investment(0)
+            for k in range(G):
+                gsend[it, k, 0:SUB] = cap[k * SUB : (k + 1) * SUB]
+                gsend[it, k, SUB : SUB + 2] = stats
+            to_peers("row", send_sums)
+            rs[it, r] = gsend[it, r]
 
         if it == 0:
             loads[3].wait()
@@ -184,41 +228,47 @@
             rx[it, r, b : b + 1, :] = row
 
         products(order, 0, tb, yv, picked, put)
-        x_sends, x_recvs = sem(1)
-
-        def send(to, device):
-            pltpu.make_async_remote_copy(
-                src_ref=rx.at[it, r], dst_ref=rx.at[it, r],
-                send_sem=x_sends, recv_sem=x_recvs, device_id=device, device_id_type=MESH,
-            ).start()
-
-        to_peers("row", send)
-
-        wait_bytes(rs.at[it, pl.ds(0, G - 1), pl.ds(0, srows)], recvs)
-        sx[it, s, 0:srows] = jnp.sum(rs[it, :, 0:srows], axis=0)
-        sends, recvs = sem(2)
-
-        def send(to, device):
-            pltpu.make_async_remote_copy(
-                src_ref=sx.at[it, s, pl.ds(0, srows)], dst_ref=sx.at[it, s, pl.ds(0, srows)],
-                send_sem=sends, recv_sem=recvs, device_id=device, device_id_type=MESH,
-            ).start()
-
-        to_peers("season", send)
-        if it == 0:
+        if it == 0:
+
+            @pl.when(early)
+            def _():
+                pl.semaphore_wait(barrier, 2 * (G - 1) + EARLY - 1)
+                to_peers("row", send_sums)
+                rs[0, r] = gsend[0, r]
+
+            @pl.when(late)
+            def _():
+                pl.semaphore_wait(barrier, 3 * (G - 1))
+                for to in range(EARLY):
+                    pl.semaphore_signal(here_sem, inc=1, device_id={"col": to}, device_id_type=MESH)
+
+        spread("row", rx.at[it, r], *sem(1))
+
+        def sum_rows():
+            wait_bytes(rs.at[it, pl.ds(0, G - 1), pl.ds(0, srows)], recv_sem.at[it, 0])
+            sx[it, s, 0:srows] = jnp.sum(rs[it, :, 0:srows], axis=0)
+            spread("season", sx.at[it, s, pl.ds(0, srows)], *sem(2))
+
+        def sum_seasons():
+            wait_bytes(sx.at[it, pl.ds(0, G - 1), pl.ds(0, srows)], recv_sem.at[it, 2])
+            return jnp.sum(sx[it, :, 0:srows], axis=0)
+
+        if it == 0:
+            pl.when(early)(sum_rows)
             for k in range(TILES):
                 t_high, t_low = split2(tiles[k].T)
                 tf[k, :, 0:TILE] = t_high
                 tf[k, :, TILE : 2 * TILE] = t_low
             for load in loads[6:]:
                 load.wait()
-        wait_bytes(rx.at[it, pl.ds(0, G - 1)], x_recvs)
+        else:
+            sum_rows()
+        wait_bytes(rx.at[it, pl.ds(0, G - 1)], recv_sem.at[it, 1])
         transposed = jnp.sum(rx[it], axis=0)
-        wait_bytes(sx.at[it, pl.ds(0, G - 1), pl.ds(0, srows)], recvs)
-        total = jnp.sum(sx[it, :, 0:srows], axis=0)
         if it == 0:
             primal_step, dual_step = jnp.full((1, 1), STEP_SCALE, F32), jnp.full((1, 1), STEP_SCALE, F32)
         else:
+            total = sum_seasons()
             dual_sq = jnp.sum(total[SUB : SUB + 1], axis=1, keepdims=True)
             primal_sq = jnp.sum(total[SUB + 1 : SUB + 2], axis=1, keepdims=True) * (1.0 / G)
             square = jnp.sqrt(primal_sq + EPSILON) * lax.rsqrt(dual_sq + EPSILON)
@@ -226,20 +276,18 @@
                 square = balance * square
             balance = jnp.sqrt(square)
             primal_step, dual_step = STEP_SCALE * lax.rsqrt(square), STEP_SCALE * balance
-
-        z_old = zv[...]
-        z_new = jnp.maximum(z_old - primal_step * (costz[...] - total[0:SUB]), 0.0)
-        zv[...] = z_new
-        ez[it, r] = 2.0 * z_new - z_old
-        sends, recvs = sem(3)
-
-        def send(to, device):
-            pltpu.make_async_remote_copy(
-                src_ref=ez.at[it, r], dst_ref=ez.at[it, r],
-                send_sem=sends, recv_sem=recvs, device_id=device, device_id_type=MESH,
-            ).start()
-
-        to_peers("row", send)
+            if it == 1:
+                @pl.when(late)
+                def _():
+                    wait_bytes(z_in, pair_sem.at[1])
+                    zv[...] = z_in[...]
+
+            z_old = zv[...]
+            z_new = jnp.maximum(z_old - primal_step * (costz[...] - total[0:SUB]), 0.0)
+            zv[...] = z_new
+            ez[it, r, 0:SUB] = 2.0 * z_new - z_old
+            spread("row", ez.at[it, r, pl.ds(0, SUB)], *sem(3))
+            z_change = jnp.sum((z_new - z_old) ** 2, axis=0, keepdims=True)
         if last:
             z_out[c, r] = z_new
             send_z(0, "col", z_out.at[c, r, TWO_STEPS])
@@ -263,33 +311,46 @@
                             send_sem=zs_sem.at[2], recv_sem=zr_sem.at[2],
                             device_id={"row": to_r, "col": to_c}, device_id_type=MESH,
                         ).start()
+        x_change = jnp.sum((x_new - x_old) ** 2, axis=0, keepdims=True)
+
+        if it == 0:
+
+            @pl.when(early)
+            def _():
+                total = sum_seasons()
+                z_old = jnp.concatenate([zv[...], z_pair[...]], axis=0)
+                cost = jnp.concatenate([costz[...], costz_pair[...]], axis=0)
+                z_new = jnp.maximum(z_old - STEP_SCALE * (cost - total), 0.0)
+                zv[...] = z_new[0:SUB]
+                z_pair[...] = z_new[SUB : 2 * SUB]
+                ez[0, r] = 2.0 * z_new - z_old
+                spread("row", ez.at[0, r], *sem(3))
+                cx[0, c, NB : NB + 1] = x_change + jnp.sum((z_new - z_old) ** 2, axis=0, keepdims=True)
+                pl.semaphore_wait(here_sem, G - EARLY)
+                z_to_pair(c + EARLY).start()
+                wait_bytes(ez.at[0, pl.ds(0, G - 1)], recv_sem.at[0, 3])
+                for (n, one), (_, two) in zip(
+                    linked(0, ez[0, :, 0:SUB].reshape(CH, TILE)),
+                    linked(1, ez[0, :, SUB : 2 * SUB].reshape(CH, TILE)),
+                ):
+                    cx[0, c, n : n + 1] = fw[n : n + 1, :] + (one + two)
+
+            @pl.when(late)
+            def _():
+                cx[0, c, 0:NB] = fw[...]
+                cx[0, c, NB : NB + 1] = x_change
+
         else:
-            cx[it, c, NB : NB + 1] = jnp.sum((x_new - x_old) ** 2, axis=0, keepdims=True) + jnp.sum(
-                (z_new - z_old) ** 2, axis=0, keepdims=True
-            )
-
-        wait_bytes(ez.at[it, pl.ds(0, G - 1)], recvs)
-        e_high, e_low = split2(ez[it].reshape(CH, TILE))
-        gathered = jnp.dot(
-            jnp.concatenate([e_high, e_low], axis=1), hot_lo[...], preferred_element_type=F32
-        )
-        for n in range(NB):
-            at = slice(n * TILE, (n + 1) * TILE)
-            linked = jnp.sum(gathered[:, at] * mask[:, at], axis=0, keepdims=True)
-            cx[it, c, n : n + 1] = fw[n : n + 1, :] + coup[n : n + 1, :] * linked
-        sends, recvs = sem(4)
-
-        def send(to, device):
-            pltpu.make_async_remote_copy(
-                src_ref=cx.at[it, c, pl.ds(0, crows)], dst_ref=cx.at[it, c, pl.ds(0, crows)],
-                send_sem=sends, recv_sem=recvs, device_id=device, device_id_type=MESH,
-            ).start()
-
-        to_peers("col", send)
+            if not last:
+                cx[it, c, NB : NB + 1] = x_change + z_change
+            wait_bytes(ez.at[it, pl.ds(0, G - 1), pl.ds(0, SUB)], recv_sem.at[it, 3])
+            for n, one in linked(0, ez[it, :, 0:SUB].reshape(CH, TILE)):
+                cx[it, c, n : n + 1] = fw[n : n + 1, :] + one
+        spread("col", cx.at[it, c, pl.ds(0, crows)], *sem(4))
         if last:
             wait_bytes(z_out.at[pl.ds(0, G - 1), 0, TWO_STEPS], zr_sem.at[0])
             send_z(1, "row", z_out.at[:, r, TWO_STEPS])
-        wait_bytes(cx.at[it, pl.ds(0, G - 1), pl.ds(0, crows)], recvs)
+        wait_bytes(cx.at[it, pl.ds(0, G - 1), pl.ds(0, crows)], recv_sem.at[it, 4])
         image = jnp.sum(cx[it, :, 0:crows], axis=0)
 
         y_old = yv[...]
@@ -308,12 +369,22 @@
     for sem in (zr_sem.at[2], zs_sem.at[2]):
         wait_bytes(rows_in.at[pl.ds(0, 3 * (G * G - 1))], sem)
     for it in range(ITERS):
-        srows = SUB if it == 0 else SUB + 2
+        srows = 2 * SUB if it == 0 else SUB + 2
+        erows = 2 * SUB if it == 0 else SUB
         crows = NB if it + 1 == ITERS else NB + 1
-        wait_bytes(gsend.at[it, pl.ds(0, G - 1), pl.ds(0, srows)], send_sem.at[it, 0])
+
+        def sent():
+            wait_bytes(gsend.at[it, pl.ds(0, G - 1), pl.ds(0, srows)], send_sem.at[it, 0])
+            wait_bytes(sx.at[it, pl.ds(0, G - 1), pl.ds(0, srows)], send_sem.at[it, 2])
+            wait_bytes(ez.at[it, pl.ds(0, G - 1), pl.ds(0, erows)], send_sem.at[it, 3])
+            if it == 0:
+                z_to_pair(c + EARLY).wait_send()
+
+        if it == 0:
+            pl.when(early)(sent)
+        else:
+            sent()
         wait_bytes(rx.at[it, pl.ds(0, G - 1)], send_sem.at[it, 1])
-        wait_bytes(sx.at[it, pl.ds(0, G - 1), pl.ds(0, srows)], send_sem.at[it, 2])
-        wait_bytes(ez.at[it, pl.ds(0, G - 1)], send_sem.at[it, 3])
         wait_bytes(cx.at[it, pl.ds(0, G - 1), pl.ds(0, crows)], send_sem.at[it, 4])
 
 
@@ -369,6 +440,9 @@
             pltpu.VMEM((NB, TILE), F32),
             pltpu.VMEM((SUB, TILE), F32),
             pltpu.VMEM((NB, TILE), F32),
+            pltpu.VMEM((SUB, TILE), F32),
+            pltpu.VMEM((SUB, TILE), F32),
+            pltpu.VMEM((SUB, TILE), F32),
             pltpu.VMEM((TILES, TILE, 2 * TILE), BF16),
             pltpu.VMEM((TILES, TILE, 2 * TILE), BF16),
             pltpu.VMEM((NB, TILE), F32),
@@ -376,23 +450,25 @@
             pltpu.VMEM((NB, 2 * TILE), F32),
             pltpu.VMEM((NB, TILE), I32),
             pltpu.SMEM((NB, TILE), I32),
-            pltpu.VMEM((CH, NB * TILE), F32),
-            pltpu.VMEM((CH, NB * TILE), BF16),
+            pltpu.VMEM((2, CH, NB * TILE), F32),
+            pltpu.VMEM((2, CH, NB * TILE), BF16),
             pltpu.VMEM((2 * TILE, NB * TILE), BF16),
-            pltpu.VMEM((2 * CH, NB * TILE), BF16),
-            pltpu.VMEM((ITERS, G, SUB + 2, TILE), F32),
-            pltpu.VMEM((ITERS, G, SUB + 2, TILE), F32),
+            pltpu.VMEM((2, 2 * CH, NB * TILE), BF16),
+            pltpu.VMEM((ITERS, G, 2 * SUB, TILE), F32),
+            pltpu.VMEM((ITERS, G, 2 * SUB, TILE), F32),
             pltpu.VMEM((ITERS, G, NB, TILE), F32),
-            pltpu.VMEM((ITERS, G, SUB + 2, TILE), F32),
-            pltpu.VMEM((ITERS, G, SUB, TILE), F32),
+            pltpu.VMEM((ITERS, G, 2 * SUB, TILE), F32),
+            pltpu.VMEM((ITERS, G, 2 * SUB, TILE), F32),
             pltpu.VMEM((ITERS, G, NB + 1, TILE), F32),
             pltpu.VMEM((3 * G * G, TILE), F32),
-            pltpu.SemaphoreType.DMA((12,)),
+            pltpu.SemaphoreType.DMA((14,)),
             pltpu.SemaphoreType.DMA,
             pltpu.SemaphoreType.DMA((ITERS, 5)),
             pltpu.SemaphoreType.DMA((ITERS, 5)),
             pltpu.SemaphoreType.DMA((3,)),
             pltpu.SemaphoreType.DMA((3,)),
+            pltpu.SemaphoreType.DMA((2,)),
+            pltpu.SemaphoreType.REGULAR,
         ],
         compiler_params=pltpu.CompilerParams(
             collective_id=0, has_side_effects=True, vmem_limit_bytes=VMEM_LIMIT

time: 70.1 us -> 67.1 us (0.957)
  Pallas kernels: 69.3 us -> 66.3 us
    pallas_call x1, Pallas kernels: 68.6 us -> 65.5 us  [local(): pl.pallas_call(kernel, out_shape=(pltpu.VMEM((NB, TILE), F32), pltpu.VMEM...]
where the time goes in v4:
time: 67.1 us; the launch traced here: 66.9 us
  Pallas kernels  66.3 us (99%)
    pallas_call x1, Pallas kernels, local(): pl.pallas_call(kernel, out_shape=(pltpu.VMEM((NB, TILE), F32), pltpu.VMEM...  65.5 us

profile of v4, /device:TPU:1, one launch (start us, length us, event | category | flops | bytes accessed | tf_op | source)
XLA Modules:
  0.0 66.9 jit_solution(7057249559082630951)
XLA Ops:
  0.6 65.5 %shard_map.139 = (f32[16,128]{1,0:T(8,128)S(1)}, f32[8,8,8,128]{3,2,1,0:T(8,128)S(1)}, f32[16,128]{1,0:T(8,128)S(1)}) custom-call(f32[32,128,128]{2,1,0:T(8,128)} %bitcast.15, s32[1,32]{1,0:T(1,128)} %bitcast.25, s32[1,32]{1,0:T(1,128)} %bitcast.26, f32[16,128]{1,0:T(8,128)} %bitcast.18, f32[16,128]{1,0:T(8,128)} %bitcast.19, s32[16,128]{1,0:T(8,128)} %bitcast.20, ...), custom_call_target="tpu_custom_call" | custom-call | tf_op jit(solution)/shard_map/pallas_call | solution.py:423
  66.2 0.7 %shard_map.140 = (f32[16,128]{1,0:T(8,128)}, f32[8,8,8,128]{3,2,1,0:T(8,128)}, f32[16,128]{1,0:T(8,128)}) custom-call(f32[16,128]{1,0:T(8,128)S(1)} %get-tuple-element.9.x_ref, f32[8,8,8,128]{3,2,1,0:T(8,128)S(1)} %get-tuple-element.10.z_ref, f32[16,128]{1,0:T(8,128)S(1)} %get-tuple-element.11.y_ref), custom_call_target="tpu_custom_call" | custom-call | tf_op jit(solution)/shard_map/pallas_call | solution.py:477

commit v5 on v4

--- a/solution.py
+++ b/solution.py
@@ -20,7 +20,8 @@
 TILES = 32
 CH = 64
 SUB = CH // G
-EARLY = 4
+EARLY = 2
+SHARE = G // EARLY
 STRAIGHT, TWO_STEPS = pl.ds(0, 3), pl.ds(3, SUB - 3)
 
 
@@ -80,15 +81,17 @@
     tiles_hbm, rows_hbm, cols_hbm, rhs_hbm, coup_hbm, asset_hbm, costx_hbm, upper_hbm, costz_hbm, x0_hbm, z0_hbm, y0_hbm,
     x_out, z_out, y_out,
     tiles, rows_ref, cols_ref, rhs_ref, coup_ref, asset_ref, costx_ref, upper_ref, costz, xv, zv, yv,
-    costz_pair, z_pair, z_in, tb, tf, tr, fw, picked, order_v, order, mask, hot_hi, hot_lo, left,
+    costz_more, z_more, z_in, tb, tf, tr, fw, picked, order_v, order, mask, hot_hi, hot_lo, left,
     gsend, rs, rx, sx, ez, cx, rows_in,
-    load_sem, order_sem, send_sem, recv_sem, zs_sem, zr_sem, pair_sem, here_sem,
+    load_sem, order_sem, send_sem, recv_sem, zs_sem, zr_sem, pair_sem, here_sem, far_sem,
 ):
     s, r, c = (lax.axis_index(a) for a in ("season", "row", "col"))
     barrier = pltpu.get_barrier_semaphore()
     early, late = c < EARLY, c >= EARLY
-    for axis in ("season", "row"):
-        for to in others(axis):
+    at_two = [lax.rem(s + k, G) for k in (2, G - 2)]
+    near = at_two + [lax.rem(s + k, G) for k in (1, G - 1)]
+    for axis, peers in (("season", near), ("row", others("row"))):
+        for to in peers:
             pl.semaphore_signal(barrier, inc=1, device_id={axis: to}, device_id_type=MESH)
     for to in others("col"):
         @pl.when(jnp.logical_or(early, to >= EARLY))
@@ -96,15 +99,15 @@
             pl.semaphore_signal(barrier, inc=1, device_id={"col": to}, device_id_type=MESH)
 
     mine = pl.ds(pl.multiple_of(c * CH + r * SUB, SUB), SUB)
-    pair = pl.ds(pl.multiple_of(lax.rem(c + EARLY, G) * CH + r * SUB, SUB), SUB)
+    more = [pl.ds(pl.multiple_of(lax.rem(c + EARLY * k, G) * CH + r * SUB, SUB), SUB) for k in range(1, SHARE)]
     loads = [
         pltpu.make_async_copy(there, here, load_sem.at[k])
         for k, (there, here) in enumerate([
             (asset_hbm, asset_ref), (coup_hbm, coup_ref), (y0_hbm, yv), (rows_hbm, rows_ref), (cols_hbm, cols_ref),
             (tiles_hbm, tiles), (costz_hbm.at[mine], costz), (z0_hbm.at[mine], zv), (x0_hbm, xv),
             (costx_hbm, costx_ref), (upper_hbm, upper_ref), (rhs_hbm, rhs_ref),
-            (costz_hbm.at[pair], costz_pair), (z0_hbm.at[pair], z_pair),
-        ])
+        ] + [(costz_hbm.at[at], costz_more.at[k]) for k, at in enumerate(more)]
+          + [(z0_hbm.at[at], z_more.at[k]) for k, at in enumerate(more)])
     ]
     for load in loads:
         load.start()
@@ -112,7 +115,6 @@
     loads[0].wait()
     asset = asset_ref[...]
     low, high = asset & (TILE - 1), (asset >> 7) - c * CH
-    high_pair = high - EARLY * CH
     for n in range(NB):
         at = slice(n * TILE, (n + 1) * TILE)
         hit = lax.broadcasted_iota(I32, (TILE, TILE), 0) == low[n : n + 1, :]
@@ -126,12 +128,13 @@
 
     @pl.when(early)
     def _():
-        for n in range(NB):
-            at = slice(n * TILE, (n + 1) * TILE)
-            hit = lax.broadcasted_iota(I32, (CH, TILE), 0) == high_pair[n : n + 1, :]
-            one = jnp.where(hit, 1.0, 0.0)
-            mask[1, :, at] = one
-            hot_hi[1, :, at] = one.astype(BF16)
+        for k in range(1, SHARE):
+            for n in range(NB):
+                at = slice(n * TILE, (n + 1) * TILE)
+                hit = lax.broadcasted_iota(I32, (CH, TILE), 0) == high[n : n + 1, :] - k * EARLY * CH
+                one = jnp.where(hit, 1.0, 0.0)
+                mask[k, :, at] = one
+                hot_hi[k, :, at] = one.astype(BF16)
 
     loads[1].wait()
     loads[2].wait()
@@ -145,14 +148,18 @@
 
         to_peers(axis, start)
 
-    def z_to_pair(to):
+    def z_to(k):
         return pltpu.make_async_remote_copy(
-            src_ref=z_pair, dst_ref=z_in, send_sem=pair_sem.at[0], recv_sem=pair_sem.at[1],
-            device_id={"col": to}, device_id_type=MESH,
+            src_ref=z_more.at[k - 1], dst_ref=z_in, send_sem=pair_sem.at[k], recv_sem=pair_sem.at[0],
+            device_id={"col": c + k * EARLY}, device_id_type=MESH,
         )
 
     def send_z(k, axis, blocks):
         spread(axis, blocks, zs_sem.at[k], zr_sem.at[k])
+
+    def vouch():
+        for to in at_two:
+            pl.semaphore_signal(far_sem, inc=1, device_id={"season": to}, device_id_type=MESH)
 
     def investment(k):
         v_high, v_low = split2(coup * yv[...])
@@ -179,7 +186,7 @@
     stats = None
     for it in range(ITERS):
         last = it + 1 == ITERS
-        srows = 2 * SUB if it == 0 else SUB + 2
+        srows = SHARE * SUB if it == 0 else SUB + 2
         crows = NB if last else NB + 1
         sem = lambda phase: (send_sem.at[it, phase], recv_sem.at[it, phase])
 
@@ -193,10 +200,14 @@
 
             @pl.when(early)
             def _():
-                for half in range(2):
+                for half in range(SHARE):
                     cap = investment(half)
                     for k in range(G):
                         gsend[0, k, half * SUB : (half + 1) * SUB] = cap[k * SUB : (k + 1) * SUB]
+                pl.semaphore_wait(barrier, len(near) + G - 1 + EARLY - 1)
+                vouch()
+                to_peers("row", send_sums)
+                rs[0, r] = gsend[0, r]
 
         else:
             cap = investment(0)
@@ -230,15 +241,10 @@
         products(order, 0, tb, yv, picked, put)
         if it == 0:
 
-            @pl.when(early)
-            def _():
-                pl.semaphore_wait(barrier, 2 * (G - 1) + EARLY - 1)
-                to_peers("row", send_sums)
-                rs[0, r] = gsend[0, r]
-
             @pl.when(late)
             def _():
-                pl.semaphore_wait(barrier, 3 * (G - 1))
+                pl.semaphore_wait(barrier, len(near) + 2 * (G - 1))
+                vouch()
                 for to in range(EARLY):
                     pl.semaphore_signal(here_sem, inc=1, device_id={"col": to}, device_id_type=MESH)
 
@@ -254,6 +260,7 @@
             return jnp.sum(sx[it, :, 0:srows], axis=0)
 
         if it == 0:
+            pl.semaphore_wait(far_sem, len(at_two))
             pl.when(early)(sum_rows)
             for k in range(TILES):
                 t_high, t_low = split2(tiles[k].T)
@@ -279,7 +286,7 @@
             if it == 1:
                 @pl.when(late)
                 def _():
-                    wait_bytes(z_in, pair_sem.at[1])
+                    wait_bytes(z_in, pair_sem.at[0])
                     zv[...] = z_in[...]
 
             z_old = zv[...]
@@ -318,22 +325,25 @@
             @pl.when(early)
             def _():
                 total = sum_seasons()
-                z_old = jnp.concatenate([zv[...], z_pair[...]], axis=0)
-                cost = jnp.concatenate([costz[...], costz_pair[...]], axis=0)
+                z_old = jnp.concatenate([zv[...]] + [z_more[k] for k in range(SHARE - 1)], axis=0)
+                cost = jnp.concatenate([costz[...]] + [costz_more[k] for k in range(SHARE - 1)], axis=0)
                 z_new = jnp.maximum(z_old - STEP_SCALE * (cost - total), 0.0)
                 zv[...] = z_new[0:SUB]
-                z_pair[...] = z_new[SUB : 2 * SUB]
+                for k in range(1, SHARE):
+                    z_more[k - 1] = z_new[k * SUB : (k + 1) * SUB]
                 ez[0, r] = 2.0 * z_new - z_old
                 spread("row", ez.at[0, r], *sem(3))
                 cx[0, c, NB : NB + 1] = x_change + jnp.sum((z_new - z_old) ** 2, axis=0, keepdims=True)
                 pl.semaphore_wait(here_sem, G - EARLY)
-                z_to_pair(c + EARLY).start()
+                for k in range(1, SHARE):
+                    z_to(k).start()
                 wait_bytes(ez.at[0, pl.ds(0, G - 1)], recv_sem.at[0, 3])
-                for (n, one), (_, two) in zip(
-                    linked(0, ez[0, :, 0:SUB].reshape(CH, TILE)),
-                    linked(1, ez[0, :, SUB : 2 * SUB].reshape(CH, TILE)),
-                ):
-                    cx[0, c, n : n + 1] = fw[n : n + 1, :] + (one + two)
+                parts = [
+                    linked(k, ez[0, :, k * SUB : (k + 1) * SUB].reshape(CH, TILE)) for k in range(SHARE)
+                ]
+                for each in zip(*parts):
+                    n = each[0][0]
+                    cx[0, c, n : n + 1] = fw[n : n + 1, :] + sum(row for _, row in each)
 
             @pl.when(late)
             def _():
@@ -369,8 +379,8 @@
     for sem in (zr_sem.at[2], zs_sem.at[2]):
         wait_bytes(rows_in.at[pl.ds(0, 3 * (G * G - 1))], sem)
     for it in range(ITERS):
-        srows = 2 * SUB if it == 0 else SUB + 2
-        erows = 2 * SUB if it == 0 else SUB
+        srows = SHARE * SUB if it == 0 else SUB + 2
+        erows = SHARE * SUB if it == 0 else SUB
         crows = NB if it + 1 == ITERS else NB + 1
 
         def sent():
@@ -378,7 +388,8 @@
             wait_bytes(sx.at[it, pl.ds(0, G - 1), pl.ds(0, srows)], send_sem.at[it, 2])
             wait_bytes(ez.at[it, pl.ds(0, G - 1), pl.ds(0, erows)], send_sem.at[it, 3])
             if it == 0:
-                z_to_pair(c + EARLY).wait_send()
+                for k in range(1, SHARE):
+                    z_to(k).wait_send()
 
         if it == 0:
             pl.when(early)(sent)
@@ -440,8 +451,8 @@
             pltpu.VMEM((NB, TILE), F32),
             pltpu.VMEM((SUB, TILE), F32),
             pltpu.VMEM((NB, TILE), F32),
-            pltpu.VMEM((SUB, TILE), F32),
-            pltpu.VMEM((SUB, TILE), F32),
+            pltpu.VMEM((SHARE - 1, SUB, TILE), F32),
+            pltpu.VMEM((SHARE - 1, SUB, TILE), F32),
             pltpu.VMEM((SUB, TILE), F32),
             pltpu.VMEM((TILES, TILE, 2 * TILE), BF16),
             pltpu.VMEM((TILES, TILE, 2 * TILE), BF16),
@@ -450,24 +461,25 @@
             pltpu.VMEM((NB, 2 * TILE), F32),
             pltpu.VMEM((NB, TILE), I32),
             pltpu.SMEM((NB, TILE), I32),
-            pltpu.VMEM((2, CH, NB * TILE), F32),
-            pltpu.VMEM((2, CH, NB * TILE), BF16),
+            pltpu.VMEM((SHARE, CH, NB * TILE), F32),
+            pltpu.VMEM((SHARE, CH, NB * TILE), BF16),
             pltpu.VMEM((2 * TILE, NB * TILE), BF16),
-            pltpu.VMEM((2, 2 * CH, NB * TILE), BF16),
-            pltpu.VMEM((ITERS, G, 2 * SUB, TILE), F32),
-            pltpu.VMEM((ITERS, G, 2 * SUB, TILE), F32),
+            pltpu.VMEM((SHARE, 2 * CH, NB * TILE), BF16),
+            pltpu.VMEM((ITERS, G, SHARE * SUB, TILE), F32),
+            pltpu.VMEM((ITERS, G, SHARE * SUB, TILE), F32),
             pltpu.VMEM((ITERS, G, NB, TILE), F32),
-            pltpu.VMEM((ITERS, G, 2 * SUB, TILE), F32),
-            pltpu.VMEM((ITERS, G, 2 * SUB, TILE), F32),
+            pltpu.VMEM((ITERS, G, SHARE * SUB, TILE), F32),
+            pltpu.VMEM((ITERS, G, SHARE * SUB, TILE), F32),
             pltpu.VMEM((ITERS, G, NB + 1, TILE), F32),
             pltpu.VMEM((3 * G * G, TILE), F32),
-            pltpu.SemaphoreType.DMA((14,)),
+            pltpu.SemaphoreType.DMA((12 + 2 * (SHARE - 1),)),
             pltpu.SemaphoreType.DMA,
             pltpu.SemaphoreType.DMA((ITERS, 5)),
             pltpu.SemaphoreType.DMA((ITERS, 5)),
             pltpu.SemaphoreType.DMA((3,)),
             pltpu.SemaphoreType.DMA((3,)),
-            pltpu.SemaphoreType.DMA((2,)),
+            pltpu.SemaphoreType.DMA((SHARE,)),
+            pltpu.SemaphoreType.REGULAR,
             pltpu.SemaphoreType.REGULAR,
         ],
         compiler_params=pltpu.CompilerParams(

time: 67.1 us -> 64.5 us (0.961)
  Pallas kernels: 66.3 us -> 63.7 us
    pallas_call x1, Pallas kernels: 65.5 us -> 62.9 us  [local(): pl.pallas_call(kernel, out_shape=(pltpu.VMEM((NB, TILE), F32), pltpu.VMEM...]
where the time goes in v5:
time: 64.5 us; the launch traced here: 64.3 us
  Pallas kernels  63.7 us (99%)
    pallas_call x1, Pallas kernels, local(): pl.pallas_call(kernel, out_shape=(pltpu.VMEM((NB, TILE), F32), pltpu.VMEM...  62.9 us

profile of v5, /device:TPU:1, one launch (start us, length us, event | category | flops | bytes accessed | tf_op | source)
XLA Modules:
  0.0 64.3 jit_solution(2647442206238518496)
XLA Ops:
  0.6 62.9 %shard_map.139 = (f32[16,128]{1,0:T(8,128)S(1)}, f32[8,8,8,128]{3,2,1,0:T(8,128)S(1)}, f32[16,128]{1,0:T(8,128)S(1)}) custom-call(f32[32,128,128]{2,1,0:T(8,128)} %bitcast.15, s32[1,32]{1,0:T(1,128)} %bitcast.25, s32[1,32]{1,0:T(1,128)} %bitcast.26, f32[16,128]{1,0:T(8,128)} %bitcast.18, f32[16,128]{1,0:T(8,128)} %bitcast.19, s32[16,128]{1,0:T(8,128)} %bitcast.20, ...), custom_call_target="tpu_custom_call" | custom-call | tf_op jit(solution)/shard_map/pallas_call | solution.py:434
  63.6 0.7 %shard_map.140 = (f32[16,128]{1,0:T(8,128)}, f32[8,8,8,128]{3,2,1,0:T(8,128)}, f32[16,128]{1,0:T(8,128)}) custom-call(f32[16,128]{1,0:T(8,128)S(1)} %get-tuple-element.9.x_ref, f32[8,8,8,128]{3,2,1,0:T(8,128)S(1)} %get-tuple-element.10.z_ref, f32[16,128]{1,0:T(8,128)S(1)} %get-tuple-element.11.y_ref), custom_call_target="tpu_custom_call" | custom-call | tf_op jit(solution)/shard_map/pallas_call | solution.py:489

commit v6 on v5

--- a/solution.py
+++ b/solution.py
@@ -83,7 +83,7 @@
     tiles, rows_ref, cols_ref, rhs_ref, coup_ref, asset_ref, costx_ref, upper_ref, costz, xv, zv, yv,
     costz_more, z_more, z_in, tb, tf, tr, fw, picked, order_v, order, mask, hot_hi, hot_lo, left,
     gsend, rs, rx, sx, ez, cx, rows_in,
-    load_sem, order_sem, send_sem, recv_sem, zs_sem, zr_sem, pair_sem, here_sem, far_sem,
+    load_sem, order_sem, send_sem, recv_sem, zs_sem, zr_sem, pair_sem, here_sem, far_sem, col_sem,
 ):
     s, r, c = (lax.axis_index(a) for a in ("season", "row", "col"))
     barrier = pltpu.get_barrier_semaphore()
@@ -94,7 +94,9 @@
         for to in peers:
             pl.semaphore_signal(barrier, inc=1, device_id={axis: to}, device_id_type=MESH)
     for to in others("col"):
-        @pl.when(jnp.logical_or(early, to >= EARLY))
+        near_col = jnp.logical_and(to >= EARLY, jnp.abs(to // 2 - c // 2) <= 1)
+
+        @pl.when(jnp.logical_or(early, near_col))
         def _():
             pl.semaphore_signal(barrier, inc=1, device_id={"col": to}, device_id_type=MESH)
 
@@ -243,8 +245,15 @@
 
             @pl.when(late)
             def _():
-                pl.semaphore_wait(barrier, len(near) + 2 * (G - 1))
+                middle = c // 2 == 2
+                pl.semaphore_wait(barrier, len(near) + G - 1 + jnp.where(middle, G - 1, G - 3))
                 vouch()
+
+                @pl.when(middle)
+                def _():
+                    for to in (c - 2, c + 2):
+                        pl.semaphore_signal(col_sem, inc=1, device_id={"col": to}, device_id_type=MESH)
+
                 for to in range(EARLY):
                     pl.semaphore_signal(here_sem, inc=1, device_id={"col": to}, device_id_type=MESH)
 
@@ -348,6 +357,11 @@
             @pl.when(late)
             def _():
                 cx[0, c, 0:NB] = fw[...]
+
+                @pl.when(c // 2 != 2)
+                def _():
+                    pl.semaphore_wait(col_sem, 1)
+
                 cx[0, c, NB : NB + 1] = x_change
 
         else:
@@ -481,6 +495,7 @@
             pltpu.SemaphoreType.DMA((SHARE,)),
             pltpu.SemaphoreType.REGULAR,
             pltpu.SemaphoreType.REGULAR,
+            pltpu.SemaphoreType.REGULAR,
         ],
         compiler_params=pltpu.CompilerParams(
             collective_id=0, has_side_effects=True, vmem_limit_bytes=VMEM_LIMIT

time: 64.5 us -> 64.4 us (level)
  no operation moved by 1% of the time
where the time goes in v6:
time: 64.4 us; the launch traced here: 64.3 us
  Pallas kernels  63.6 us (99%)
    pallas_call x1, Pallas kernels, local(): pl.pallas_call(kernel, out_shape=(pltpu.VMEM((NB, TILE), F32), pltpu.VMEM...  62.9 us

profile of v6, /device:TPU:1, one launch (start us, length us, event | category | flops | bytes accessed | tf_op | source)
XLA Modules:
  0.0 64.3 jit_solution(1010920035876313069)
XLA Ops:
  0.6 62.9 %shard_map.139 = (f32[16,128]{1,0:T(8,128)S(1)}, f32[8,8,8,128]{3,2,1,0:T(8,128)S(1)}, f32[16,128]{1,0:T(8,128)S(1)}) custom-call(f32[32,128,128]{2,1,0:T(8,128)} %bitcast.15, s32[1,32]{1,0:T(1,128)} %bitcast.25, s32[1,32]{1,0:T(1,128)} %bitcast.26, f32[16,128]{1,0:T(8,128)} %bitcast.18, f32[16,128]{1,0:T(8,128)} %bitcast.19, s32[16,128]{1,0:T(8,128)} %bitcast.20, ...), custom_call_target="tpu_custom_call" | custom-call | tf_op jit(solution)/shard_map/pallas_call | solution.py:448
  63.5 0.7 %shard_map.140 = (f32[16,128]{1,0:T(8,128)}, f32[8,8,8,128]{3,2,1,0:T(8,128)}, f32[16,128]{1,0:T(8,128)}) custom-call(f32[16,128]{1,0:T(8,128)S(1)} %get-tuple-element.9.x_ref, f32[8,8,8,128]{3,2,1,0:T(8,128)S(1)} %get-tuple-element.10.z_ref, f32[16,128]{1,0:T(8,128)S(1)} %get-tuple-element.11.y_ref), custom_call_target="tpu_custom_call" | custom-call | tf_op jit(solution)/shard_map/pallas_call | solution.py:504
